TPU v7x, 32 devices: a whole 2x2x4 slice. The times are simulated.
32 devices in a mesh: grp: 2 (over y), gx: 16 (over z, x, core).
Axes of the slice: x: 2, y: 2, z: 4, core: 2. Of those that a mesh axis runs over, the one named last changes fastest.
Arguments:
- features: bfloat16 [128, 32, 64, 128], P('grp', 'gx'), parts along dimension 0, may hold values from -6 to 6
- cotangent: bfloat16 [128, 32, 64, 128], P('grp', 'gx'), parts along dimension 0, may hold values from -6 to 6
- spectral_weight: bfloat16 [16384, 64, 128], P('gx'), may hold values from -0.5 to 0.5
- channel_weight: bfloat16 [64, 64], replicated, may hold values from -0.75 to 0.75
- channel_bias: float32 [64], replicated, may hold values from -3 to 3
Outputs:
- activated: bfloat16 [128, 32, 64, 128], P('grp', 'gx'), parts along dimension 0
- feature_grad: bfloat16 [128, 32, 64, 128], P('grp', 'gx'), parts along dimension 0
- spectral_grad: bfloat16 [32768, 64, 128], P(('grp', 'gx')), parts along dimension 0
There are 2 independent parts, one for each index of `grp`. A program takes and returns all parts, laid end to end along the dimension named above; an argument that names none is the same for every part. Nothing has to cross between parts.
All inputs are finite; a program needn't handle non-finite values.
Results may differ from a plain program's by a relative error of at most 0.018.
Values may be sent and summed in bfloat16 or wider, within the bound.
A program may use at most 192 MiB of HBM per device.

v0:
```python
import functools
import math

import jax
import jax.numpy as jnp
from jax import lax
from jax.experimental import pallas as pl
from jax.experimental.pallas import tpu as pltpu
from jax.sharding import PartitionSpec as P

MX = 32
MY = 32
MZ = 16


SQRT_TWO_PI = math.sqrt(2.0 / math.pi)
CUBIC_COEF = 0.044715


def freq_index(retained, length):
    ladder = jnp.arange(retained, dtype=jnp.int32)
    return jnp.where(ladder < retained // 2, ladder, length - retained + ladder)


def cos_sin(wavenum, length):
    points = jnp.arange(length, dtype=jnp.int32)
    angles = (wavenum[:, None] * points[None, :] % length).astype(jnp.float32) * (
        2.0 * math.pi / length
    )
    return (jnp.cos(angles), jnp.sin(angles))


def analysis_pair(wavenum, length):
    cosine, sine_wave = cos_sin(wavenum, length)
    cosine, sine_wave = (cosine.T, sine_wave.T)
    return jnp.stack(
        [jnp.stack([cosine, -sine_wave], 1), jnp.stack([sine_wave, cosine], 1)], 1
    ).astype(jnp.bfloat16)


def synthesis_pair(wavenum, length):
    cosine, sine_wave = cos_sin(wavenum, length)
    return jnp.stack(
        [jnp.stack([cosine, sine_wave], 1), jnp.stack([-sine_wave, cosine], 1)], 1
    ).astype(jnp.bfloat16)


def depth_table(retained, length):
    cosine, sine_wave = cos_sin(jnp.arange(retained, dtype=jnp.int32), length)
    return jnp.concatenate([cosine, -sine_wave], 0).astype(jnp.bfloat16)


def gelu_parts(inputs):
    squared = inputs * inputs
    slope = SQRT_TWO_PI * CUBIC_COEF
    tangent = jnp.tanh(inputs * (SQRT_TWO_PI + slope * squared))
    half = 0.5 + 0.5 * tangent
    output = inputs * half
    derivative = half + output * (1.0 - tangent) * (SQRT_TWO_PI + 3.0 * slope * squared)
    return (output, derivative)


def mode_product(coeffs, weights):
    channels = weights.shape[1]
    halves = jnp.einsum("mac,mcj->amj", coeffs, weights, preferred_element_type=jnp.float32)
    real_out = halves[0, :, :channels] - halves[1, :, channels:]
    imag_out = halves[0, :, channels:] + halves[1, :, :channels]
    return jnp.stack([real_out, imag_out], 1).astype(jnp.bfloat16)


def exchange(blocks):
    return lax.all_to_all(blocks, "gx", 0, 0, tiled=True)


def middle_kernel(
    scale, feat_ref, cot_ref, lines_ref, weight_ref, bias_ref, basis_ref, act_ref, up_ref, grad_ref
):
    channels, _, rows, depth_len = feat_ref.shape
    spectral = jnp.dot(
        lines_ref[0].reshape(rows * channels, lines_ref.shape[3]),
        basis_ref[...],
        preferred_element_type=jnp.float32,
    ).reshape(rows, channels, depth_len)
    feats = jnp.swapaxes(feat_ref[:, 0].astype(jnp.float32), 0, 1).astype(jnp.bfloat16)
    cots = jnp.swapaxes(cot_ref[:, 0].astype(jnp.float32), 0, 1)
    acts = []
    for row in range(rows):
        pointwise = jnp.dot(weight_ref[...], feats[row], preferred_element_type=jnp.float32)
        hidden = spectral[row] * scale + pointwise + bias_ref[...]
        activated, derivative = gelu_parts(hidden)
        acts.append(activated)
        up_ref[0, row] = (cots[row] * derivative).astype(jnp.bfloat16)
    act_ref[:, 0] = jnp.swapaxes(jnp.stack(acts, 0), 0, 1).astype(jnp.bfloat16)
    grad = lax.dot_general(
        up_ref[0].reshape(rows * channels, depth_len),
        basis_ref[...],
        (((1,), (1,)), ((), ())),
        preferred_element_type=jnp.float32,
    )
    grad_ref[0] = (grad * scale).astype(jnp.bfloat16).reshape(rows, channels, lines_ref.shape[3])


def final_kernel(up_ref, depth_ref, weight_ref, basis_ref, out_ref):
    _, rows, channels, depth_len = up_ref.shape
    spectral = jnp.dot(
        depth_ref[0].reshape(rows * channels, depth_ref.shape[3]),
        basis_ref[...],
        preferred_element_type=jnp.float32,
    ).reshape(rows, channels, depth_len)
    totals = []
    for row in range(rows):
        back = jnp.dot(weight_ref[...], up_ref[0, row], preferred_element_type=jnp.float32)
        totals.append(spectral[row] + back)
    out_ref[:, 0] = jnp.swapaxes(jnp.stack(totals, 0), 0, 1).astype(jnp.bfloat16)


ROWS = 16


def middle(features, cotangent, lines_back, channel_weight, channel_bias, depth_basis, scale):
    channels, planes, lines, depth_len = features.shape
    parts = lines_back.shape[3]
    field = pl.BlockSpec((channels, 1, ROWS, depth_len), lambda x, y: (0, x, y, 0))
    turned = pl.BlockSpec((1, ROWS, channels, depth_len), lambda x, y: (x, y, 0, 0))
    narrow = pl.BlockSpec((1, ROWS, channels, parts), lambda x, y: (x, y, 0, 0))
    count = features.size
    return pl.pallas_call(
        functools.partial(middle_kernel, scale),
        grid=(planes, lines // ROWS),
        in_specs=[
            field,
            field,
            narrow,
            pl.BlockSpec((channels, channels), lambda x, y: (0, 0)),
            pl.BlockSpec((channels, 1), lambda x, y: (0, 0)),
            pl.BlockSpec((parts, depth_len), lambda x, y: (0, 0)),
        ],
        out_specs=[field, turned, narrow],
        out_shape=[
            jax.ShapeDtypeStruct(features.shape, jnp.bfloat16),
            jax.ShapeDtypeStruct((planes, lines, channels, depth_len), jnp.bfloat16),
            jax.ShapeDtypeStruct((planes, lines, channels, parts), jnp.bfloat16),
        ],
        compiler_params=pltpu.CompilerParams(vmem_limit_bytes=56 * 1024 * 1024),
        cost_estimate=pl.CostEstimate(
            flops=count * 2 * (channels + 2 * parts), bytes_accessed=count * 8, transcendentals=count
        ),
    )(features, cotangent, lines_back, channel_weight, channel_bias[:, None], depth_basis)


def final(upstream, depth_grad, weight_back, depth_basis):
    planes, lines, channels, depth_len = upstream.shape
    parts = depth_grad.shape[3]
    count = upstream.size
    return pl.pallas_call(
        final_kernel,
        grid=(planes, lines // ROWS),
        in_specs=[
            pl.BlockSpec((1, ROWS, channels, depth_len), lambda x, y: (x, y, 0, 0)),
            pl.BlockSpec((1, ROWS, channels, parts), lambda x, y: (x, y, 0, 0)),
            pl.BlockSpec((channels, channels), lambda x, y: (0, 0)),
            pl.BlockSpec((parts, depth_len), lambda x, y: (0, 0)),
        ],
        out_specs=pl.BlockSpec((channels, 1, ROWS, depth_len), lambda x, y: (0, x, y, 0)),
        out_shape=jax.ShapeDtypeStruct((channels, planes, lines, depth_len), jnp.bfloat16),
        compiler_params=pltpu.CompilerParams(vmem_limit_bytes=32 * 1024 * 1024),
        cost_estimate=pl.CostEstimate(
            flops=count * 2 * (channels + parts), bytes_accessed=count * 4, transcendentals=0
        ),
    )(upstream, depth_grad, weight_back, depth_basis)


def body(features, cotangent, spectral_weight, channel_weight, channel_bias):
    channels, planes, lines, depth_len = features.shape
    devices = lax.axis_size("gx")
    all_planes = planes * devices
    owned_modes = spectral_weight.shape[0]
    wave_pairs = MY * MZ
    owned_pairs = owned_modes // MX
    wide = 2 * channels
    forward_scale = 1.0 / math.sqrt(all_planes * lines * depth_len)
    inverse_scale = 1.0 / math.sqrt(MX * wave_pairs)
    weight_scale = math.sqrt(MX * wave_pairs / (all_planes * lines * depth_len))
    depth_basis = depth_table(MZ, depth_len)
    across_y = analysis_pair(freq_index(MY, lines), lines)
    back_y = synthesis_pair(freq_index(MY, lines), lines)
    across_x = analysis_pair(freq_index(MX, all_planes), all_planes)
    back_x = synthesis_pair(freq_index(MX, all_planes), all_planes)

    def to_owners(rows):
        blocks = rows.reshape(devices, owned_pairs * planes, wide)
        return exchange(blocks).reshape(devices, owned_pairs, planes, 2, channels)

    def to_planes(rows):
        blocks = rows.reshape(devices, planes * owned_pairs, wide)
        got = exchange(blocks).reshape(devices, planes, owned_pairs, 2, channels)
        return got.transpose(1, 0, 2, 3, 4).reshape(planes, MY, MZ, 2, channels)

    depth_part = jnp.dot(features, depth_basis.T, preferred_element_type=jnp.float32).astype(
        jnp.bfloat16
    )
    plane_part = jnp.einsum(
        "cxyaz,yabk->kzxbc",
        depth_part.reshape(channels, planes, lines, 2, MZ),
        across_y,
        preferred_element_type=jnp.float32,
    ).astype(jnp.bfloat16)
    gathered = to_owners(plane_part)
    mode_sums = jnp.einsum(
        "sqpac,spabk->qkbc",
        gathered,
        across_x.reshape(devices, planes, 2, 2, MX),
        preferred_element_type=jnp.float32,
    )
    coeffs = (mode_sums * forward_scale).astype(jnp.bfloat16).reshape(owned_modes, 2, channels)
    spectral = mode_product(coeffs, spectral_weight)
    planes_back = jnp.einsum(
        "qkao,kabx->xqbo",
        spectral.reshape(owned_pairs, MX, 2, channels),
        back_x,
        preferred_element_type=jnp.float32,
    ).astype(jnp.bfloat16)
    planes_here = to_planes(planes_back)
    lines_back = (
        jnp.einsum("xkzao,kaby->xyobz", planes_here, back_y, preferred_element_type=jnp.float32)
        .astype(jnp.bfloat16)
        .reshape(planes, lines, channels, 2 * MZ)
    )
    activated, upstream, lines_grad = middle(
        features, cotangent, lines_back, channel_weight, channel_bias, depth_basis, inverse_scale
    )
    rows_grad = jnp.einsum(
        "xyobz,kaby->kzxao",
        lines_grad.reshape(planes, lines, channels, 2, MZ),
        back_y,
        preferred_element_type=jnp.float32,
    ).astype(jnp.bfloat16)
    gathered_grad = to_owners(rows_grad)
    grad_modes = (
        jnp.einsum(
            "sqpbo,kabsp->qkao",
            gathered_grad,
            back_x.reshape(MX, 2, 2, devices, planes),
            preferred_element_type=jnp.float32,
        )
        .astype(jnp.bfloat16)
        .reshape(owned_modes, 2, channels)
    )
    straight = grad_modes.reshape(owned_modes, wide)
    rotated = jnp.concatenate([grad_modes[:, 1], -grad_modes[:, 0]], 1)
    pairs = jnp.stack([straight, rotated], 1)
    coeff_grad = (
        jnp.einsum("mcj,mbj->mbc", spectral_weight, pairs, preferred_element_type=jnp.float32)
        * forward_scale
    ).astype(jnp.bfloat16)
    plane_grad = jnp.einsum(
        "qkbc,xabk->xqac",
        coeff_grad.reshape(owned_pairs, MX, 2, channels),
        across_x,
        preferred_element_type=jnp.float32,
    ).astype(jnp.bfloat16)
    grad_here = to_planes(plane_grad)
    spectral_grad = (
        jnp.einsum("mac,maj->mcj", coeffs, pairs, preferred_element_type=jnp.float32)
        * weight_scale
    ).astype(jnp.bfloat16)
    depth_grad = (
        jnp.einsum("xkzbc,yabk->xycaz", grad_here, across_y, preferred_element_type=jnp.float32)
        .astype(jnp.bfloat16)
        .reshape(planes, lines, channels, 2 * MZ)
    )
    feature_grad = final(upstream, depth_grad, channel_weight.T, depth_basis)
    return (activated, feature_grad, spectral_grad)


def solution(mesh):
    in_specs = (
        P("grp", "gx", None, None),
        P("grp", "gx", None, None),
        P("gx", None, None),
        P(),
        P(),
    )
    out_specs = (
        P("grp", "gx", None, None),
        P("grp", "gx", None, None),
        P(("grp", "gx"), None, None),
    )
    return jax.shard_map(body, mesh=mesh, in_specs=in_specs, out_specs=out_specs, check_vma=False)
```

profile of v0, /device:TPU:0, one launch (start us, length us, event | category | flops | bytes accessed | tf_op | source)
XLA Modules:
  0.0 122.0 jit_solution(4302214794336831756)
XLA Ops:
  0.9 3.7 %convolution_convert_fusion = bf16[32,64,2,64]{3,0,2,1:T(8,128)(2,1)S(1)} fusion(bf16[64,2,64,128]{3,2,1,0:T(8,128)(2,1)} %feat_ref.1, bf16[16,128]{1,0:T(8,128)(2,1)S(1)} %get-tuple-element.35, bf16[16,128]{1,0:T(8,128)(2,1)S(1)} %get-tuple-element.36), kind=kOutput, calls=%fused_computation.3 | convolution fusion | flops 67387392 | bytes 2629632 | tf_op jit(solution)/shard_map/dot_general | solution.py:199
  4.5 1.4 %fusion.13 = bf16[32,16,2,2,64]{4,0,1,2,3:T(8,128)(2,1)S(1)} fusion(bf16[64,2,64,2,16]{2,4,3,1,0:T(8,128)(2,1)S(1)} %bitcast.196, bf16[64,1,2,32]{0,3,1,2:T(8,128)(2,1)S(1)} %get-tuple-element.22, bf16[64,1,2,32]{0,3,1,2:T(8,128)(2,1)S(1)} %get-tuple-element.21), kind=kOutput, calls=%fused_computation.25 | convolution fusion | flops 33718272 | bytes 802816 | tf_op jit(solution)/shard_map/cxyaz,yabk->kzxbc/dot_general | solution.py:202
  6.5 1.0 reshape.548
  7.4 7.4 %all-to-all-start = ((bf16[16,64,128]{2,1,0:T(8,128)(2,1)}), bf16[16,64,128]{2,1,0:T(8,128)(2,1)S(1)}, u32[]{:S(2)}, u32[]{:S(2)}) async-start(bf16[16,64,128]{2,1,0:T(8,128)(2,1)} %reshape.548), calls=%async_computation | async-start | bytes 524288 | tf_op jit(solution)/shard_map/all_to_all | solution.py:72
  15.2 9.7 %all-to-all-done = bf16[16,64,128]{2,1,0:T(8,128)(2,1)S(1)} async-done(((bf16[16,64,128]{2,1,0:T(8,128)(2,1)}), bf16[16,64,128]{2,1,0:T(8,128)(2,1)S(1)}, u32[]{:S(2)}, u32[]{:S(2)}) %all-to-all-start) | async-done | bytes 262176 | tf_op jit(solution)/shard_map/all_to_all | solution.py:72
  25.6 8.1 %convolution_bitcast_fusion.5 = f32[2,1024,128]{2,0,1:T(2,128)S(1)} fusion(bf16[1024,64,128]{2,1,0:T(8,128)(2,1)} %param.7, bf16[1024,2,64]{2,0,1:T(8,128)(2,1)S(1)} %bitcast.199), kind=kOutput, calls=%fused_computation.11 | convolution fusion | flops 33554432 | bytes 18087936 | tf_op jit(solution)/shard_map/mac,mcj->amj/dot_general | solution.py:65
  33.7 2.3 %fusion.19 = (bf16[1,1024,64]{2,0,1:T(2,128)(2,1)S(1)}, bf16[1,1024,64]{2,0,1:T(2,128)(2,1)S(1)}) fusion(f32[2,1024,128]{2,0,1:T(2,128)S(1)} %convolution_bitcast_fusion.5), kind=kLoop, calls=%fused_computation.33 | loop fusion | flops 262144 | bytes 1310720 | tf_op jit(solution)/shard_map/convert.17
  37.1 1.0 reshape.551
  38.0 3.7 %all-to-all-start.1 = ((bf16[16,64,128]{2,1,0:T(8,128)(2,1)}), bf16[16,64,128]{2,1,0:T(8,128)(2,1)S(1)}, u32[]{:S(2)}, u32[]{:S(2)}) async-start(bf16[16,64,128]{2,1,0:T(8,128)(2,1)} %reshape.551), calls=%async_computation.1 | async-start | bytes 524288 | tf_op jit(solution)/shard_map/all_to_all | solution.py:72
  41.8 0.7 copy.39.bias_ref
  43.2 8.4 %all-to-all-done.1 = bf16[16,64,128]{2,1,0:T(8,128)(2,1)S(1)} async-done(((bf16[16,64,128]{2,1,0:T(8,128)(2,1)}), bf16[16,64,128]{2,1,0:T(8,128)(2,1)S(1)}, u32[]{:S(2)}, u32[]{:S(2)}) %all-to-all-start.1) | async-done | bytes 262176 | tf_op jit(solution)/shard_map/all_to_all | solution.py:72
  53.1 1.8 %copy.38.lines_ref = bf16[2,64,64,32]{3,2,1,0:T(8,128)(2,1)} copy(bf16[2,64,64,32]{2,3,1,0:T(8,128)(2,1)S(1)} %bitcast.197) | data formatting | bytes 1048576 | tf_op jit(solution)/shard_map/reshape | solution.py:227
  54.9 11.0 %shard_map.76 = (bf16[64,2,64,128]{3,2,1,0:T(8,128)(2,1)}, bf16[2,64,64,128]{3,2,1,0:T(8,128)(2,1)}, bf16[2,64,64,32]{3,2,1,0:T(8,128)(2,1)}) custom-call(bf16[64,2,64,128]{3,2,1,0:T(8,128)(2,1)} %feat_ref.1, bf16[64,2,64,128]{3,2,1,0:T(8,128)(2,1)} %cot_ref.1, bf16[2,64,64,32]{3,2,1,0:T(8,128)(2,1)} %copy.38.lines_ref, bf16[64,64]{1,0:T(8,128)(2,1)} %weight_ref.1, ...), custom_call_target="tpu_custom_call" | custom-call | flops 268435456 | bytes 8388608 | tf_op jit(solution)/shard_map/pallas_call | solution.py:127
  65.9 2.0 %copy.40 = bf16[2,64,64,32]{2,3,1,0:T(8,128)(2,1)S(1)} copy(bf16[2,64,64,32]{3,2,1,0:T(8,128)(2,1)} %get-tuple-element.8) | data formatting | bytes 1048576 | tf_op jit(solution)/shard_map/pallas_call | solution.py:127
  68.9 1.0 reshape.556
  69.9 3.5 %all-to-all-start.2 = ((bf16[16,64,128]{2,1,0:T(8,128)(2,1)}), bf16[16,64,128]{2,1,0:T(8,128)(2,1)S(1)}, u32[]{:S(2)}, u32[]{:S(2)}) async-start(bf16[16,64,128]{2,1,0:T(8,128)(2,1)} %reshape.556), calls=%async_computation.2 | async-start | bytes 524288 | tf_op jit(solution)/shard_map/all_to_all | solution.py:72
  73.7 9.7 %all-to-all-done.2 = bf16[16,64,128]{2,1,0:T(8,128)(2,1)S(1)} async-done(((bf16[16,64,128]{2,1,0:T(8,128)(2,1)}), bf16[16,64,128]{2,1,0:T(8,128)(2,1)S(1)}, u32[]{:S(2)}, u32[]{:S(2)}) %all-to-all-start.2) | async-done | bytes 262176 | tf_op jit(solution)/shard_map/all_to_all | solution.py:72
  85.7 12.3 %fusion.7 = bf16[1024,2,64]{2,1,0:T(2,128)(2,1)S(1)} fusion(bf16[1024,64,128]{2,1,0:T(8,128)(2,1)} %param.7, bf16[1024,1,128]{2,1,0:T(2,128)(2,1)S(1)} %copy.47, bf16[1024,1,128]{2,1,0:T(2,128)(2,1)S(1)} %stack_reshape_reshape.4), kind=kOutput, calls=%fused_computation.19 | convolution fusion | flops 34865152 | bytes 17563648 | tf_op jit(solution)/shard_map/mcj,mbj->mbc/dot_general | solution.py:253
  98.9 1.0 reshape.560
  99.9 3.8 %all-to-all-start.3 = ((bf16[16,64,128]{2,1,0:T(8,128)(2,1)}), bf16[16,64,128]{2,1,0:T(8,128)(2,1)S(1)}, u32[]{:S(2)}, u32[]{:S(2)}) async-start(bf16[16,64,128]{2,1,0:T(8,128)(2,1)} %reshape.560), calls=%async_computation.3 | async-start | bytes 524288 | tf_op jit(solution)/shard_map/all_to_all | solution.py:72
  103.6 9.5 %multiply_convert_fusion = bf16[1024,64,128]{2,1,0:T(8,128)(2,1)} fusion(bf16[1024,2,64]{2,0,1:T(8,128)(2,1)S(1)} %bitcast.200, bf16[1024,1,128]{2,1,0:T(2,128)(2,1)S(1)} %copy.47, bf16[1024,1,128]{2,1,0:T(2,128)(2,1)S(1)} %stack_reshape_reshape.4), kind=kOutput, calls=%fused_computation | convolution fusion | flops 51380224 | bytes 17563648 | tf_op jit(solution)/shard_map/mac,maj->mcj/dot_general | solution.py:264
  114.9 1.0 copy.56.depth_ref
  116.0 1.6 %copy-done = bf16[2,64,64,128]{3,2,1,0:T(8,128)(2,1)S(1)} copy-done((bf16[2,64,64,128]{3,2,1,0:T(8,128)(2,1)S(1)}, bf16[2,64,64,128]{3,2,1,0:T(8,128)(2,1)}, u32[]{:S(2)}) %copy-start) | copy-done | bytes 2097176
  117.6 4.4 %shard_map.77 = bf16[64,2,64,128]{3,2,1,0:T(8,128)(2,1)} custom-call(bf16[2,64,64,128]{3,2,1,0:T(8,128)(2,1)S(1)} %copy-done, bf16[2,64,64,32]{3,2,1,0:T(8,128)(2,1)S(1)} %copy.56.depth_ref, bf16[64,64]{1,0:T(8,128)(2,1)S(1)} %bitcast.191, bf16[32,128]{1,0:T(8,128)(2,1)S(1)} %copy-done.1), custom_call_target="tpu_custom_call" | custom-call | flops 201326592 | bytes 4194304 | tf_op jit(solution)/shard_map/pallas_call | solution.py:155
  (48 shorter events, 11.2 us)
Async XLA Ops:
  7.4 17.4 %all-to-all-start = ((bf16[16,64,128]{2,1,0:T(8,128)(2,1)}), bf16[16,64,128]{2,1,0:T(8,128)(2,1)S(1)}, u32[]{:S(2)}, u32[]{:S(2)}) async-start(bf16[16,64,128]{2,1,0:T(8,128)(2,1)} %reshape.548), calls=%async_computation | async-start | bytes 524288 | tf_op jit(solution)/shard_map/all_to_all | solution.py:72
  36.1 5.6 %copy-start.3 = (f32[64]{0:T(128)S(1)}, f32[64]{0:T(128)}, u32[]{:S(2)}) copy-start(f32[64]{0:T(128)} %param.9) | copy-start | bytes 772
  38.0 13.5 %all-to-all-start.1 = ((bf16[16,64,128]{2,1,0:T(8,128)(2,1)}), bf16[16,64,128]{2,1,0:T(8,128)(2,1)S(1)}, u32[]{:S(2)}, u32[]{:S(2)}) async-start(bf16[16,64,128]{2,1,0:T(8,128)(2,1)} %reshape.551), calls=%async_computation.1 | async-start | bytes 524288 | tf_op jit(solution)/shard_map/all_to_all | solution.py:72
  67.9 5.6 %copy-start.2 = (bf16[64,64]{1,0:T(8,128)(2,1)S(1)}, bf16[64,64]{1,0:T(8,128)(2,1)}, u32[]{:S(2)}) copy-start(bf16[64,64]{1,0:T(8,128)(2,1)} %weight_ref.1) | copy-start | bytes 24580
  69.9 13.5 %all-to-all-start.2 = ((bf16[16,64,128]{2,1,0:T(8,128)(2,1)}), bf16[16,64,128]{2,1,0:T(8,128)(2,1)S(1)}, u32[]{:S(2)}, u32[]{:S(2)}) async-start(bf16[16,64,128]{2,1,0:T(8,128)(2,1)} %reshape.556), calls=%async_computation.2 | async-start | bytes 524288 | tf_op jit(solution)/shard_map/all_to_all | solution.py:72
  99.9 13.5 %all-to-all-start.3 = ((bf16[16,64,128]{2,1,0:T(8,128)(2,1)}), bf16[16,64,128]{2,1,0:T(8,128)(2,1)S(1)}, u32[]{:S(2)}, u32[]{:S(2)}) async-start(bf16[16,64,128]{2,1,0:T(8,128)(2,1)} %reshape.560), calls=%async_computation.3 | async-start | bytes 524288 | tf_op jit(solution)/shard_map/all_to_all | solution.py:72
  114.9 1.1 copy-start.1
  116.0 1.6 %copy-start = (bf16[2,64,64,128]{3,2,1,0:T(8,128)(2,1)S(1)}, bf16[2,64,64,128]{3,2,1,0:T(8,128)(2,1)}, u32[]{:S(2)}) copy-start(bf16[2,64,64,128]{3,2,1,0:T(8,128)(2,1)} %get-tuple-element.7.up_ref) | copy-start | bytes 6291460
where the time goes:
time: 123 us; the launch traced here: 122 us
  matrix products  38.1 us (31%)
  waiting for transfers between devices  28.1 us (23%)
  starting transfers between devices  18.4 us (15%)
  local copies, waits for them, and re-layouts  17.1 us (14%)
  Pallas kernels  15.4 us (13%)
  other arithmetic  4.03 us (3%)
    all_to_all x4, waiting for transfers between devices, exchange(): return lax.all_to_all(blocks, 'gx', 0, 0, tiled=True)  28.1 us
    all_to_all x4, starting transfers between devices, exchange(): return lax.all_to_all(blocks, 'gx', 0, 0, tiled=True)  18.4 us
    dot_general x1, matrix products, body(): jnp.einsum('mcj,mbj->mbc', spectral_weight, pairs, preferred_element_type...  12.3 us
    pallas_call x1, Pallas kernels, middle(): pl.pallas_call(functools.partial(middle_kernel, scale), grid=(planes, lin...  11 us
    dot_general x1, matrix products, body(): jnp.einsum('mac,maj->mcj', coeffs, pairs, preferred_element_type=jnp.floa...  9.49 us
    dot_general x1, matrix products, mode_product(): jnp.einsum('mac,mcj->amj', coeffs, weights, preferred_element_type=jnp.fl...  8.14 us
    pallas_call x1, Pallas kernels, final(): pl.pallas_call(final_kernel, grid=(planes, lines // ROWS), in_specs=[pl.B...  4.42 us
    dot_general x1, matrix products, body(): jnp.dot(features, depth_basis.T, preferred_element_type=jnp.float32)  3.66 us
  transfers between devices with their start and end apart: 4, of which 4 were waited for; matrix products, arithmetic and copies ran while one was open for 9% of the time, Pallas kernels for 0%

commit v1 on v0

--- a/solution.py
+++ b/solution.py
@@ -3,6 +3,7 @@
 
 import jax
 import jax.numpy as jnp
+import numpy as np
 from jax import lax
 from jax.experimental import pallas as pl
 from jax.experimental.pallas import tpu as pltpu
@@ -170,7 +171,7 @@
     )(upstream, depth_grad, weight_back, depth_basis)
 
 
-def body(features, cotangent, spectral_weight, channel_weight, channel_bias):
+def plain_body(features, cotangent, spectral_weight, channel_weight, channel_bias):
     channels, planes, lines, depth_len = features.shape
     devices = lax.axis_size("gx")
     all_planes = planes * devices
@@ -273,6 +274,702 @@
     return (activated, feature_grad, spectral_grad)
 
 
+MESH = pl.DeviceIdType.MESH
+F32 = jnp.float32
+BF16 = jnp.bfloat16
+MB = 1024 * 1024
+
+
+def host_cos_sin(wavenum, length):
+    angles = (np.outer(wavenum, np.arange(length)) % length).astype(np.float32) * np.float32(
+        2.0 * math.pi / length
+    )
+    return np.cos(angles), np.sin(angles)
+
+
+def host_freq(retained, length):
+    ladder = np.arange(retained)
+    return np.where(ladder < retained // 2, ladder, length - retained + ladder)
+
+
+def host_minus(retained, length):
+    cosine, sine = host_cos_sin(host_freq(retained, length), length)
+    cosine, sine = cosine.T, sine.T
+    return np.stack([np.stack([cosine, -sine], 1), np.stack([sine, cosine], 1)], 1)
+
+
+def host_plus(retained, length):
+    cosine, sine = host_cos_sin(host_freq(retained, length), length)
+    return np.stack([np.stack([cosine, sine], 1), np.stack([-sine, cosine], 1)], 1)
+
+
+def host_tables(devices, lines, depth_len, channels):
+    all_planes = 2 * devices
+    two = np.eye(2)
+    eight = np.eye(8)
+    cosine, sine = host_cos_sin(np.arange(MZ), depth_len)
+    depth = np.stack([cosine, -sine], 0)
+    z_in = np.einsum("akz,cd->czakd", depth, eight).reshape(8 * depth_len, 16 * MZ)
+    minus_y = host_minus(MY, lines).reshape(lines, 2, 2, devices, 2)
+    y_in = np.einsum("yabdk,xw->dkbwxay", minus_y, two).reshape(8 * devices, 4 * lines)
+    groups = channels // 8
+    source = np.arange(MZ * channels).reshape(groups, MZ, 8)
+    target = source.transpose(1, 0, 2).reshape(-1)
+    order = np.zeros((MZ * channels, MZ * channels))
+    order[target, np.arange(MZ * channels)] = 1.0
+    minus_x = host_minus(MX, all_planes).reshape(devices, 2, 2, 2, MX)
+    x_in = np.einsum("sxabk,hg,jl,p->hkjpbsglax", minus_x, two, two, np.ones(2)).reshape(
+        16 * MX, 16 * devices
+    )
+    swapped = np.stack([minus_x[:, :, :, 1], -minus_x[:, :, :, 0]], 3)
+    x_turn = np.einsum("sxabk,hg,jl,p->hkjpbsglax", swapped, two, two, np.ones(2)).reshape(
+        16 * MX, 16 * devices
+    )
+    plus_x = host_plus(MX, all_planes).reshape(MX, 2, 2, devices, 2)
+    crossed = np.stack([-plus_x[:, :, 1], plus_x[:, :, 0]], 2)
+    both = np.stack([plus_x, crossed], 0)
+    x_out = np.einsum("rkabsx,pq,jl->prsjbxklqa", both, two, two).reshape(32 * devices, 8 * MX)
+    x_back = np.einsum("kabsx,jl,q->sjbxklqa", plus_x, two, np.ones(2)).reshape(
+        8 * devices, 8 * MX
+    )
+    plus_y = host_plus(MY, lines).reshape(devices, 2, 2, 2, lines)
+    y_out = np.einsum("skaby,hg,xw->xbhysgkaw", plus_y, two, two).reshape(8 * lines, 16 * devices)
+    tables = dict(
+        z_in=z_in, z_out=z_in.T, y_in=y_in, order=order, unorder=order.T, x_in=x_in,
+        x_turn=x_turn, x_out=x_out, x_back=x_back, y_out=y_out,
+    )
+    return {name: jnp.asarray(np.ascontiguousarray(t), BF16) for name, t in tables.items()}
+
+
+def fdot(left, right):
+    return jnp.dot(left, right, preferred_element_type=F32)
+
+
+def greet(devices):
+    me, group = lax.axis_index("gx"), lax.axis_index("grp")
+    barrier = pltpu.get_barrier_semaphore()
+
+    @pl.loop(1, devices)
+    def _(step):
+        pl.semaphore_signal(
+            barrier, inc=1, device_id=(group, lax.rem(me + step, devices)), device_id_type=MESH
+        )
+
+    def arrived():
+        pl.semaphore_wait(barrier, devices - 1)
+
+    return arrived
+
+
+def swap_start(devices, sent, got, send_sem, recv_sem, stage):
+    me, group = lax.axis_index("gx"), lax.axis_index("grp")
+
+    def copy(step):
+        target = lax.rem(me + step, devices)
+        return pltpu.make_async_remote_copy(
+            src_ref=sent.at[target],
+            dst_ref=got.at[me],
+            send_sem=send_sem.at[stage, step],
+            recv_sem=recv_sem.at[stage, step],
+            device_id=(group, target),
+            device_id_type=MESH,
+        )
+
+    @pl.loop(1, devices)
+    def _(step):
+        copy(step).start()
+
+    got[me] = sent[me]
+
+    def finish():
+        @pl.loop(1, devices)
+        def _(step):
+            copy(step).wait_recv()
+
+    def drained():
+        @pl.loop(1, devices)
+        def _(step):
+            copy(step).wait_send()
+
+    return finish, drained
+
+
+def to_chunks(devices, lines_ref, y_in, order, sent):
+    rows = fdot(y_in[...], lines_ref[...]).astype(BF16)
+    rows = fdot(rows, order[...])
+    lanes = rows.shape[1]
+    halves = [
+        rows[:, h * lanes // 2 : (h + 1) * lanes // 2].reshape(devices, 8, lanes // 2)
+        for h in range(2)
+    ]
+    chunk = jnp.concatenate(halves, 1).astype(BF16)
+    for u in range(2):
+        sent[u] = chunk[:, :, u * lanes // 4 : (u + 1) * lanes // 4]
+
+
+def mode_block(weights, k_pair, half, pair):
+    def one(kx):
+        return jnp.concatenate(
+            [weights[k2, half * 8 + pair * 2 + parity, kx] for k2 in range(2) for parity in range(2)],
+            0,
+        )
+
+    return jnp.concatenate([one(2 * k_pair), one(2 * k_pair + 1)], 1)
+
+
+def iotas():
+    row = lax.broadcasted_iota(jnp.int32, (8, 128), 0)
+    lane = lax.broadcasted_iota(jnp.int32, (8, 128), 1)
+    return row, lane
+
+
+def weight_copies(weights_hbm, weights, sem):
+    def copy(half, pair):
+        kz = pl.ds(half * 8 + pair * 2, 2)
+        return pltpu.make_async_copy(
+            weights_hbm.at[:, kz], weights.at[:, kz], sem.at[half, pair]
+        )
+
+    return copy
+
+
+def fill_kron(channel_weight, out, contract):
+    size = out.shape[0]
+    channels = channel_weight.shape[0]
+
+    def spread(rows, first, axis):
+        shape = (rows, channels) if axis == 0 else (channels, rows)
+        long = lax.broadcasted_iota(jnp.int32, shape, axis)
+        short = lax.broadcasted_iota(jnp.int32, shape, 1 - axis)
+        return jnp.where(long // 16 + first == short, 1.0, 0.0).astype(BF16)
+
+    columns = spread(size, 0, 1)
+    line = lax.broadcasted_iota(jnp.int32, (128, size), 0) % 16
+    same = line == lax.broadcasted_iota(jnp.int32, (128, size), 1) % 16
+
+    @pl.loop(0, size // 128)
+    def _(block):
+        rows = lax.dot_general(
+            spread(128, block * 8, 0),
+            channel_weight[...],
+            (((1,), (1 - contract,)), ((), ())),
+            preferred_element_type=F32,
+        ).astype(BF16)
+        out[pl.ds(pl.multiple_of(block * 128, 128), 128), :] = jnp.where(
+            same, fdot(rows, columns), 0.0
+        ).astype(BF16)
+
+
+def enter_kernel(
+    devices, forward_scale,
+    feat_hbm, weights_hbm, channel_weight, z_in, y_in, order, x_in, x_out,
+    got_out, back_out, kron_hbm, kron_back_hbm,
+    feat, weights, lines_part, sent, got, modes, mixed, sent_back, got_back, krons,
+    feat_sem, weight_sem, kron_sem, send_sem, recv_sem,
+):
+    channels, planes, lines, depth_len = feat.shape
+    groups = channels // 8
+    arrived = greet(devices)
+    load = pltpu.make_async_copy(feat_hbm, feat, feat_sem)
+    load.start()
+    load.wait()
+    weight_copy = weight_copies(weights_hbm, weights, weight_sem)
+    for pair in range(4):
+        for half in range(2):
+            weight_copy(half, pair).start()
+
+    @pl.loop(0, groups)
+    def _(group):
+        for plane in range(planes):
+            wide = jnp.concatenate([feat[group * 8 + i, plane] for i in range(8)], 1)
+            part = fdot(wide, z_in[...]).astype(BF16)
+            for a in range(2):
+                lines_part[
+                    pl.ds((plane * 2 + a) * lines, lines),
+                    pl.ds(pl.multiple_of(group * 128, 128), 128),
+                ] = part[:, a * 128 : (a + 1) * 128]
+
+    to_chunks(devices, lines_part, y_in, order, sent)
+    arrived()
+    ends = [
+        swap_start(devices, sent.at[u], got.at[u], send_sem, recv_sem, u) for u in range(2)
+    ]
+    kron_copies = []
+    for back in range(2):
+        fill_kron(channel_weight, krons.at[back], 1 - back)
+        kron_copies.append(
+            pltpu.make_async_copy(
+                krons.at[back], [kron_hbm, kron_back_hbm][back], kron_sem.at[back]
+            )
+        )
+        kron_copies[back].start()
+    row, lane = iotas()
+    own = [(row // 2) == (lane // 64 + 2 * k2) for k2 in range(2)]
+    low = lax.broadcasted_iota(jnp.int32, (8 * devices, 128), 1) < 64
+    for u in range(2):
+        ends[u][0]()
+        source = got[u].reshape(16 * devices, 256)
+        modes[...] = (fdot(x_in[...], source) * forward_scale).reshape(2, MX, 8, 256)
+
+        @pl.loop(0, 4)
+        def _(part):
+            half, local = part // 2, part % 2
+            weight_copy(half, 2 * u + local).wait()
+            span = pl.ds(pl.multiple_of(local * 128, 128), 128)
+
+            def step(k_pair, carry):
+                left = []
+                for i in range(2):
+                    block = modes[half, 2 * k_pair + i, :, span]
+                    left.append(
+                        jnp.concatenate([jnp.where(own[0], block, 0.0), jnp.where(own[1], block, 0.0)], 1)
+                    )
+                left = jnp.concatenate(left, 0).astype(BF16)
+                out = fdot(left, mode_block(weights, k_pair, half, 2 * u + local))
+                out = jnp.concatenate([out[:8, :128], out[8:, 128:]], 0).astype(BF16)
+                mixed[half, pl.ds(pl.multiple_of(k_pair * 16, 16), 16), span] = out
+                return carry
+
+            lax.fori_loop(0, MX // 2, step, 0, unroll=8)
+
+        halves = []
+        for half in range(2):
+            every = fdot(x_out[...], mixed[half])
+            size = 8 * devices
+            tiles = []
+            for local in range(2):
+                even, even_x, odd, odd_x = [
+                    every[i * size : (i + 1) * size, local * 128 : (local + 1) * 128]
+                    for i in range(4)
+                ]
+                tiles.append(
+                    jnp.where(low, even, odd_x) + pltpu.roll(jnp.where(low, odd, even_x), 64, 1)
+                )
+            halves.append(jnp.concatenate(tiles, 1).reshape(devices, 8, 256))
+        sent_back[u] = jnp.concatenate(halves, 1).astype(BF16)
+        ends.append(swap_start(devices, sent_back.at[u], got_back.at[u], send_sem, recv_sem, 2 + u))
+    got_out[...] = got[...]
+    for copy in kron_copies:
+        copy.wait()
+    ends[2][0]()
+    ends[3][0]()
+    for end in ends:
+        end[1]()
+    back_out[...] = got_back[...]
+
+
+def middle_transform(devices, back, y_out, unorder, blocks):
+    lines_u = [fdot(y_out[...], back[u].reshape(16 * devices, 256)).astype(BF16) for u in range(2)]
+    lines = lines_u[0].shape[0] // 8
+    for plane in range(2):
+        for part in range(2):
+            pieces = []
+            for half in range(2):
+                first = ((plane * 2 + part) * 2 + half) * lines
+                pieces += [lines_u[u][first : first + lines] for u in range(2)]
+            rows = fdot(jnp.concatenate(pieces, 1), unorder[...]).astype(BF16)
+            groups = rows.shape[1] // 128
+            for block in range(lines // 16):
+                for group in range(groups):
+                    blocks[
+                        block,
+                        (plane * groups + group) * 16 : (plane * groups + group + 1) * 16,
+                        part * 128 : (part + 1) * 128,
+                    ] = rows[block * 16 : (block + 1) * 16, group * 128 : (group + 1) * 128]
+
+
+def new_middle_kernel(
+    devices, scale,
+    feat, cot, back, kron, bias, z_in, z_out, y_in, y_out, order, unorder,
+    act, up, chunks,
+    blocks, lines_part, pointwise, spectral, up_wide,
+):
+    channels, planes, rows, depth_len = feat.shape
+    groups = channels // 8
+    step = pl.program_id(0)
+
+    @pl.when(step == 0)
+    def _():
+        middle_transform(devices, back, y_out, unorder, blocks)
+
+    spectral[...] = fdot(blocks[step], z_out[...])
+    both = jnp.concatenate(
+        [feat[:, x].reshape(channels * rows, depth_len) for x in range(planes)], 1
+    )
+    pointwise[...] = fdot(kron[...], both)
+
+    @pl.loop(0, groups)
+    def _(group):
+        for plane in range(planes):
+            here = pl.ds(pl.multiple_of((plane * groups + group) * rows, 16), rows)
+            for i in range(8):
+                o = group * 8 + i
+                hidden = (
+                    spectral[here, i * 128 : (i + 1) * 128] * scale
+                    + pointwise[pl.ds(pl.multiple_of(o * rows, 16), rows), plane * 128 : (plane + 1) * 128]
+                    + bias[o]
+                )
+                activated, derivative = gelu_parts(hidden)
+                act[o, plane] = activated.astype(BF16)
+                upstream = (cot[o, plane].astype(F32) * derivative).astype(BF16)
+                up[o, plane] = upstream
+                up_wide[here, i * 128 : (i + 1) * 128] = upstream
+
+    grad = (fdot(up_wide[...], z_in[...]) * scale).astype(BF16)
+    for plane in range(planes):
+        for a in range(2):
+            first = (plane * 2 + a) * 64
+            for group in range(groups):
+                lines_part[
+                    pl.ds(pl.multiple_of(first + step * rows, 16), rows),
+                    group * 128 : (group + 1) * 128,
+                ] = grad[
+                    (plane * groups + group) * rows : (plane * groups + group + 1) * rows,
+                    a * 128 : (a + 1) * 128,
+                ]
+
+    @pl.when(step == pl.num_programs(0) - 1)
+    def _():
+        to_chunks(devices, lines_part, y_in, order, chunks)
+
+
+def return_kernel(
+    devices, forward_scale,
+    sent_in, weights_hbm, x_in, x_turn, x_back,
+    got_out, back_out,
+    weights, sent, got, modes, turned, mixed, sent_back, got_back,
+    weight_sem, send_sem, recv_sem,
+):
+    arrived = greet(devices)
+    weight_copy = weight_copies(weights_hbm, weights, weight_sem)
+    for pair in range(4):
+        for half in range(2):
+            weight_copy(half, pair).start()
+    sent[...] = sent_in[...]
+    arrived()
+    ends = [
+        swap_start(devices, sent.at[u], got.at[u], send_sem, recv_sem, u) for u in range(2)
+    ]
+    row, lane = iotas()
+    low = lane < 64
+    direct = low == ((row // 2) % 2 == 0)
+    first_line = row < 4
+    zero = jnp.zeros((8, 128), F32)
+    for u in range(2):
+        ends[u][0]()
+        source = got[u].reshape(16 * devices, 256)
+        modes[...] = fdot(x_in[...], source).reshape(2, MX, 8, 256)
+        turned[...] = fdot(x_turn[...], source).reshape(2, MX, 8, 256)
+
+        @pl.loop(0, 4)
+        def _(part):
+            half, local = part // 2, part % 2
+            weight_copy(half, 2 * u + local).wait()
+            span = pl.ds(pl.multiple_of(local * 128, 128), 128)
+
+            def step(k_pair, carry):
+                pairs = []
+                for i in range(2):
+                    straight = modes[half, 2 * k_pair + i, :, span]
+                    other = turned[half, 2 * k_pair + i, :, span]
+                    pairs.append(pair_tile(straight, other, low, direct))
+                left = jnp.concatenate(
+                    [jnp.concatenate([pairs[0], zero], 1), jnp.concatenate([zero, pairs[1]], 1)], 0
+                ).astype(BF16)
+                out = lax.dot_general(
+                    left,
+                    mode_block(weights, k_pair, half, 2 * u + local),
+                    (((1,), (1,)), ((), ())),
+                    preferred_element_type=F32,
+                )
+                tiles = []
+                for i in range(2):
+                    rows = out[8 * i : 8 * i + 8]
+                    tiles.append(
+                        jnp.where(direct, jnp.where(first_line, rows[:, :128], rows[:, 128:]), 0.0)
+                    )
+                mixed[half, pl.ds(pl.multiple_of(k_pair * 16, 16), 16), span] = (
+                    jnp.concatenate(tiles, 0) * forward_scale
+                ).astype(BF16)
+                return carry
+
+            lax.fori_loop(0, MX // 2, step, 0, unroll=8)
+
+        sent_back[u] = jnp.concatenate(
+            [fdot(x_back[...], mixed[half]).reshape(devices, 8, 256) for half in range(2)], 1
+        ).astype(BF16)
+        ends.append(swap_start(devices, sent_back.at[u], got_back.at[u], send_sem, recv_sem, 2 + u))
+    got_out[...] = got[...]
+    ends[2][0]()
+    ends[3][0]()
+    for end in ends:
+        end[1]()
+    back_out[...] = got_back[...]
+
+
+def pair_tile(straight, other, low, direct):
+    return jnp.where(
+        direct,
+        jnp.where(low, straight, other),
+        pltpu.roll(jnp.where(low, other, straight), 64, 1),
+    )
+
+
+def weight_grad_kernel(
+    devices, forward_scale, weight_scale,
+    got, got_grad, x_in, x_turn,
+    out_hbm,
+    coeffs, modes, turned, buffer, sem,
+):
+    row, lane = iotas()
+    low = lane < 64
+    direct = low == ((row // 2) % 2 == 0)
+    own = [(row // 2) == (lane // 64 + 2 * k2) for k2 in range(2)]
+    for u in range(2):
+        coeffs[u] = (fdot(x_in[...], got[u].reshape(16 * devices, 256)) * forward_scale).reshape(
+            2, MX, 8, 256
+        )
+        source = got_grad[u].reshape(16 * devices, 256)
+        modes[u] = fdot(x_in[...], source).reshape(2, MX, 8, 256)
+        turned[u] = fdot(x_turn[...], source).reshape(2, MX, 8, 256)
+    block = lax.broadcasted_iota(jnp.int32, (128, 256), 0) // 8
+    side = lax.broadcasted_iota(jnp.int32, (128, 256), 1) // 128
+
+    def copy(index, slot):
+        return pltpu.make_async_copy(
+            buffer.at[slot], out_hbm.at[:, pl.ds(2 * index, 2)], sem.at[slot]
+        )
+
+    @pl.loop(0, 8)
+    def _(index):
+        slot = lax.rem(index, 2)
+        half, u, local = index // 4, (index % 4) // 2, index % 2
+        span = pl.ds(pl.multiple_of(local * 128, 128), 128)
+
+        @pl.when(index >= 2)
+        def _():
+            copy(index - 2, slot).wait()
+
+        @pl.loop(0, 2)
+        def _(k_half):
+            here = pl.ds(k_half * (MX // 2), MX // 2)
+            values = coeffs[u, half, here, :, span]
+            wide = jnp.concatenate(
+                [jnp.where(own[k2][None], values, 0.0).reshape(128, 128) for k2 in range(2)], 1
+            )
+            left = wide.T.astype(BF16)
+            pairs = []
+            for k in range(MX // 2):
+                pairs.append(
+                    pair_tile(
+                        modes[u, half, k_half * (MX // 2) + k, :, span],
+                        turned[u, half, k_half * (MX // 2) + k, :, span],
+                        low,
+                        direct,
+                    )
+                )
+            pairs = jnp.concatenate(pairs, 0).astype(BF16).astype(F32) * weight_scale
+            pairs = jnp.concatenate([pairs, pairs], 1)
+            for i in range(MX // 4):
+                right = jnp.where(block == 2 * i + side, pairs, 0.0).astype(BF16)
+                out = fdot(left, right).astype(BF16)
+                for s in range(2):
+                    for k2 in range(2):
+                        for parity in range(2):
+                            first = (k2 * 2 + parity) * 64
+                            buffer[slot, k2, parity, k_half * (MX // 2) + 2 * i + s] = out[
+                                first : first + 64, s * 128 : (s + 1) * 128
+                            ]
+
+        copy(index, slot).start()
+
+    copy(6, 0).wait()
+    copy(7, 1).wait()
+
+
+def new_final_kernel(devices, up, back, kron, z_out, y_out, unorder, out, blocks, pointwise, spectral):
+    channels, planes, rows, depth_len = up.shape
+    groups = channels // 8
+    step = pl.program_id(0)
+
+    @pl.when(step == 0)
+    def _():
+        middle_transform(devices, back, y_out, unorder, blocks)
+
+    spectral[...] = fdot(blocks[step], z_out[...])
+    both = jnp.concatenate(
+        [up[:, x].reshape(channels * rows, depth_len) for x in range(planes)], 1
+    )
+    pointwise[...] = fdot(kron[...], both)
+
+    @pl.loop(0, groups)
+    def _(group):
+        for plane in range(planes):
+            here = pl.ds(pl.multiple_of((plane * groups + group) * rows, 16), rows)
+            for i in range(8):
+                o = group * 8 + i
+                total = (
+                    spectral[here, i * 128 : (i + 1) * 128]
+                    + pointwise[pl.ds(pl.multiple_of(o * rows, 16), rows), plane * 128 : (plane + 1) * 128]
+                )
+                out[o, plane] = total.astype(BF16)
+
+
+def vmem(*shape, dtype=BF16):
+    return pltpu.VMEM(shape, dtype)
+
+
+WHOLE = pl.BlockSpec(memory_space=pltpu.VMEM)
+ANYWHERE = pl.BlockSpec(memory_space=pl.ANY)
+
+
+def block_body(features, cotangent, spectral_weight, channel_weight, channel_bias):
+    channels, planes, lines, depth_len = features.shape
+    devices = lax.axis_size("gx")
+    all_planes = planes * devices
+    number = MX * MY * MZ
+    forward_scale = 1.0 / math.sqrt(all_planes * lines * depth_len)
+    inverse_scale = 1.0 / math.sqrt(number)
+    weight_scale = math.sqrt(number / (all_planes * lines * depth_len))
+    tables = host_tables(devices, lines, depth_len, channels)
+    weights = spectral_weight.reshape(2, MZ, MX, channels, 2 * channels)
+    wide = MZ * channels
+    chunk = jax.ShapeDtypeStruct((2, devices, 16, 256), BF16)
+    dma = pltpu.SemaphoreType.DMA
+    square = jax.ShapeDtypeStruct((16 * channels, 16 * channels), BF16)
+    got, back, kron, kron_back = pl.pallas_call(
+        functools.partial(enter_kernel, devices, forward_scale),
+        out_shape=[chunk, chunk, square, square],
+        in_specs=[ANYWHERE, ANYWHERE] + [WHOLE] * 6,
+        out_specs=[WHOLE, WHOLE, ANYWHERE, ANYWHERE],
+        scratch_shapes=[
+            vmem(*features.shape),
+            vmem(*weights.shape),
+            vmem(4 * lines, wide),
+            vmem(*chunk.shape),
+            vmem(*chunk.shape),
+            vmem(2, MX, 8, 256, dtype=F32),
+            vmem(2, 8 * MX, 256),
+            vmem(*chunk.shape),
+            vmem(*chunk.shape),
+            vmem(2, *square.shape),
+            dma(()),
+            dma((2, 4)),
+            dma((2,)),
+            dma((4, devices)),
+            dma((4, devices)),
+        ],
+        compiler_params=pltpu.CompilerParams(
+            collective_id=0, has_side_effects=True, vmem_limit_bytes=48 * MB
+        ),
+        name="enter",
+    )(
+        features, weights, channel_weight, tables["z_in"], tables["y_in"], tables["order"],
+        tables["x_in"], tables["x_out"],
+    )
+    rows = 16
+    field = pl.BlockSpec((channels, planes, rows, depth_len), lambda y: (0, 0, y, 0))
+
+    def full(array):
+        return pl.BlockSpec(array.shape, lambda y: (0,) * len(array.shape))
+
+    like = jax.ShapeDtypeStruct(features.shape, BF16)
+    activated, upstream, sent = pl.pallas_call(
+        functools.partial(new_middle_kernel, devices, inverse_scale),
+        grid=(lines // rows,),
+        in_specs=[
+            field, field, full(chunk), full(kron), pl.BlockSpec(memory_space=pltpu.SMEM),
+            full(tables["z_in"]), full(tables["z_out"]), full(tables["y_in"]),
+            full(tables["y_out"]), full(tables["order"]), full(tables["unorder"]),
+        ],
+        out_specs=[field, field, full(chunk)],
+        out_shape=[like, like, chunk],
+        scratch_shapes=[
+            vmem(lines // rows, 2 * wide // 8, 256),
+            vmem(4 * lines, wide),
+            vmem(channels * rows, planes * depth_len, dtype=F32),
+            vmem(planes * channels * 2, 8 * depth_len, dtype=F32),
+            vmem(planes * channels * 2, 8 * depth_len),
+        ],
+        compiler_params=pltpu.CompilerParams(vmem_limit_bytes=48 * MB),
+        name="middle",
+    )(
+        features, cotangent, back, kron, channel_bias, tables["z_in"], tables["z_out"],
+        tables["y_in"], tables["y_out"], tables["order"], tables["unorder"],
+    )
+    got_grad, back_grad = pl.pallas_call(
+        functools.partial(return_kernel, devices, forward_scale),
+        out_shape=[chunk, chunk],
+        in_specs=[WHOLE, ANYWHERE] + [WHOLE] * 3,
+        out_specs=[WHOLE, WHOLE],
+        scratch_shapes=[
+            vmem(*weights.shape),
+            vmem(*chunk.shape),
+            vmem(*chunk.shape),
+            vmem(2, MX, 8, 256, dtype=F32),
+            vmem(2, MX, 8, 256, dtype=F32),
+            vmem(2, 8 * MX, 256),
+            vmem(*chunk.shape),
+            vmem(*chunk.shape),
+            dma((2, 4)),
+            dma((4, devices)),
+            dma((4, devices)),
+        ],
+        compiler_params=pltpu.CompilerParams(
+            collective_id=1, has_side_effects=True, vmem_limit_bytes=48 * MB
+        ),
+        name="backward",
+    )(sent, weights, tables["x_in"], tables["x_turn"], tables["x_back"])
+    spectral_grad = pl.pallas_call(
+        functools.partial(weight_grad_kernel, devices, forward_scale, weight_scale),
+        out_shape=jax.ShapeDtypeStruct(weights.shape, BF16),
+        in_specs=[WHOLE] * 4,
+        out_specs=ANYWHERE,
+        scratch_shapes=[
+            vmem(2, 2, MX, 8, 256, dtype=F32),
+            vmem(2, 2, MX, 8, 256, dtype=F32),
+            vmem(2, 2, MX, 8, 256, dtype=F32),
+            vmem(2, 2, 2, MX, channels, 2 * channels),
+            dma((2,)),
+        ],
+        compiler_params=pltpu.CompilerParams(vmem_limit_bytes=40 * MB),
+        name="weight_grad",
+    )(got, got_grad, tables["x_in"], tables["x_turn"])
+    feature_grad = pl.pallas_call(
+        functools.partial(new_final_kernel, devices),
+        grid=(lines // rows,),
+        in_specs=[
+            field, full(chunk), full(kron), full(tables["z_out"]), full(tables["y_out"]),
+            full(tables["unorder"]),
+        ],
+        out_specs=field,
+        out_shape=like,
+        scratch_shapes=[
+            vmem(lines // rows, 2 * wide // 8, 256),
+            vmem(channels * rows, planes * depth_len, dtype=F32),
+            vmem(planes * channels * 2, 8 * depth_len, dtype=F32),
+        ],
+        compiler_params=pltpu.CompilerParams(vmem_limit_bytes=40 * MB),
+        name="final",
+    )(upstream, back_grad, kron_back, tables["z_out"], tables["y_out"], tables["unorder"])
+    return (activated, feature_grad, spectral_grad.reshape(spectral_weight.shape))
+
+
+def body(features, cotangent, spectral_weight, channel_weight, channel_bias):
+    channels, planes, lines, depth_len = features.shape
+    devices = lax.axis_size("gx")
+    fits = (
+        2 * devices == MY
+        and planes == 2
+        and channels == 64
+        and lines == 64
+        and depth_len == 128
+        and spectral_weight.shape[0] == 2 * MZ * MX
+    )
+    chosen = block_body if fits else plain_body
+    return chosen(features, cotangent, spectral_weight, channel_weight, channel_bias)
+
+
 def solution(mesh):
     in_specs = (
         P("grp", "gx", None, None),

time: 123 us -> 90.3 us (0.73)
  Pallas kernels: 15.4 us -> 83.3 us
  matrix products: 38.1 us -> 0 us
  waiting for transfers between devices: 28.1 us -> 0 us
  starting transfers between devices: 18.4 us -> 0 us
  local copies, waits for them, and re-layouts: 17.1 us -> 5.86 us
  other arithmetic: 4.03 us -> 0 us
    pallas_call x2 -> x5, Pallas kernels: 15.4 us -> 83.3 us  [the longest x1 27.6 us: block_body(): pl.pallas_call(functools.partial(enter_kernel, devices, forward_scale), o...]
    dot_general x12 -> x0, matrix products: 38.1 us -> none  [the longest x1 12.3 us: body(): jnp.einsum('mcj,mbj->mbc', spectral_weight, pairs, preferred_element_type...]
    all_to_all x4 -> x0, waiting for transfers between devices: 28.1 us -> none  [exchange(): return lax.all_to_all(blocks, 'gx', 0, 0, tiled=True)]
    all_to_all x4 -> x0, starting transfers between devices: 18.4 us -> none  [exchange(): return lax.all_to_all(blocks, 'gx', 0, 0, tiled=True)]
    reshape x12 -> x0, local copies, waits for them, and re-layouts: 7.79 us -> none  [the longest x2 1.91 us: to_planes(): blocks = rows.reshape(devices, planes * owned_pairs, wide)]
    unnamed x11 -> x32, local copies, waits for them, and re-layouts: 1.76 us -> 5.86 us
    convert_element_type x7 -> x0, local copies, waits for them, and re-layouts: 4.06 us -> none  [the longest x1 0.68 us: body(): lines_back = jnp.einsum('xkzao,kaby->xyobz', planes_here, back_y, preferr...]
    another operation x12 -> x0, other arithmetic: 3.38 us -> none
  transfers between devices with their start and end apart: 4 -> 0, of which waited for: 4 -> 0; matrix products, arithmetic and copies ran while one was open for 9% -> 0% of each run, Pallas kernels for 0% -> 0%
where the time goes in v1:
time: 90.3 us; the launch traced here: 90 us
  Pallas kernels  83.3 us (92%)
  local copies, waits for them, and re-layouts  5.86 us (6%)
    pallas_call x1, Pallas kernels, block_body(): pl.pallas_call(functools.partial(enter_kernel, devices, forward_scale), o...  27.6 us
    pallas_call x1, Pallas kernels, block_body(): pl.pallas_call(functools.partial(return_kernel, devices, forward_scale),...  22.4 us
    pallas_call x1, Pallas kernels, block_body(): pl.pallas_call(functools.partial(new_middle_kernel, devices, inverse_scal...  15.6 us
    pallas_call x1, Pallas kernels, block_body(): pl.pallas_call(functools.partial(weight_grad_kernel, devices, forward_sca...  10.9 us
    pallas_call x1, Pallas kernels, block_body(): pl.pallas_call(functools.partial(new_final_kernel, devices), grid=(lines...  6.87 us
    unnamed x32, local copies, waits for them, and re-layouts  5.86 us

profile of v1, /device:TPU:0, one launch (start us, length us, event | category | flops | bytes accessed | tf_op | source)
XLA Modules:
  0.0 90.0 jit_solution(1089009029254321502)
XLA Ops:
  0.6 0.0 copy-start.2
  0.6 0.9 %copy-done.2 = bf16[512,256]{1,0:T(8,128)(2,1)S(1)} copy-done((bf16[512,256]{1,0:T(8,128)(2,1)S(1)}, bf16[512,256]{1,0:T(8,128)(2,1)}, u32[]{:S(2)}) %copy-start.2) | copy-done | bytes 262168
  1.6 1.0 %copy-done.5 = bf16[1024,256]{1,0:T(8,128)(2,1)S(1)} copy-done((bf16[1024,256]{1,0:T(8,128)(2,1)S(1)}, bf16[1024,256]{1,0:T(8,128)(2,1)}, u32[]{:S(2)}) %copy-start.5) | copy-done | bytes 524312
  2.6 0.9 %copy-done.10 = bf16[512,256]{1,0:T(8,128)(2,1)S(1)} copy-done((bf16[512,256]{1,0:T(8,128)(2,1)S(1)}, bf16[512,256]{1,0:T(8,128)(2,1)}, u32[]{:S(2)}) %copy-start.10) | copy-done | bytes 262168
  3.6 0.8 copy-done.11
  4.4 0.7 copy-done.14
  5.1 0.0 copy-start.12
  5.2 0.0 copy-start.15
  5.2 27.6 %enter.1 = (bf16[2,16,16,256]{3,2,1,0:T(8,128)(2,1)S(1)}, bf16[2,16,16,256]{3,2,1,0:T(8,128)(2,1)S(1)}, bf16[1024,1024]{1,0:T(8,128)(2,1)S(1)}, bf16[1024,1024]{1,0:T(8,128)(2,1)S(1)}) custom-call(bf16[64,2,64,128]{3,2,1,0:T(8,128)(2,1)} %feat.1, bf16[2,16,32,64,128]{4,3,2,1,0:T(8,128)(2,1)} %bitcast.2, bf16[64,64]{1,0:T(8,128)(2,1)S(1)} %copy-done.14, ...), custom_call_target="tpu_custom_call" | custom-call | tf_op jit(solution)/shard_map/enter/pallas_call | solution.py:840
  32.8 0.0 copy-start.7
  32.8 1.3 %copy-done.7 = bf16[1024,1024]{1,0:T(8,128)(2,1)} copy-done((bf16[1024,1024]{1,0:T(8,128)(2,1)}, bf16[1024,1024]{1,0:T(8,128)(2,1)S(1)}, u32[]{:S(2)}) %copy-start.7) | copy-done | bytes 2097176
  34.1 0.0 copy-done
  34.1 0.0 copy-done.4
  34.1 0.0 copy-done.6
  34.1 0.0 copy-done.9
  34.1 0.0 copy-start.3
  34.1 0.0 copy-start.8
  34.1 0.0 copy-start.13
  34.2 15.6 %middle.1 = (bf16[64,2,64,128]{3,2,1,0:T(8,128)(2,1)}, bf16[64,2,64,128]{3,2,1,0:T(8,128)(2,1)S(1)}, bf16[2,16,16,256]{3,2,1,0:T(8,128)(2,1)S(1)}) custom-call(bf16[64,2,64,128]{3,2,1,0:T(8,128)(2,1)S(1)} %copy-done, bf16[64,2,64,128]{3,2,1,0:T(8,128)(2,1)} %cot.1, bf16[2,16,16,256]{3,2,1,0:T(8,128)(2,1)S(1)} %get-tuple-element.12.back, ...), custom_call_target="tpu_custom_call" | custom-call | tf_op jit(solution)/shard_map/middle/pallas_call | solution.py:877
  49.7 0.0 copy-done.13
  49.8 0.0 copy-start.1
  49.8 22.4 %backward.1 = (bf16[2,16,16,256]{3,2,1,0:T(8,128)(2,1)S(1)}, bf16[2,16,16,256]{3,2,1,0:T(8,128)(2,1)S(1)}) custom-call(bf16[2,16,16,256]{3,2,1,0:T(8,128)(2,1)S(1)} %get-tuple-element.16.sent_in, bf16[2,16,32,64,128]{4,3,2,1,0:T(8,128)(2,1)} %bitcast.3, bf16[512,256]{1,0:T(8,128)(2,1)S(1)} %copy-done.3, bf16[512,256]{1,0:T(8,128)(2,1)S(1)} %copy-done.8, ...), custom_call_target="tpu_custom_call" | custom-call | tf_op jit(solution)/shard_map/backward/pallas_call | solution.py:900
  72.2 6.9 %final.1 = bf16[64,2,64,128]{3,2,1,0:T(8,128)(2,1)} custom-call(bf16[64,2,64,128]{3,2,1,0:T(8,128)(2,1)S(1)} %get-tuple-element.15.up, bf16[2,16,16,256]{3,2,1,0:T(8,128)(2,1)S(1)} %get-tuple-element.17.back, bf16[1024,1024]{1,0:T(8,128)(2,1)S(1)} %get-tuple-element.18.kron, bf16[256,1024]{1,0:T(8,128)(2,1)S(1)} %copy-done.4, ...), custom_call_target="tpu_custom_call" | custom-call | tf_op jit(solution)/shard_map/final/pallas_call | solution.py:938
  79.1 10.9 %weight_grad.1 = bf16[2,16,32,64,128]{4,3,2,1,0:T(8,128)(2,1)} custom-call(bf16[2,16,16,256]{3,2,1,0:T(8,128)(2,1)S(1)} %get-tuple-element.19.got, bf16[2,16,16,256]{3,2,1,0:T(8,128)(2,1)S(1)} %get-tuple-element.20.got_grad, bf16[512,256]{1,0:T(8,128)(2,1)S(1)} %copy-done.3, bf16[512,256]{1,0:T(8,128)(2,1)S(1)} %copy-done.8), custom_call_target="tpu_custom_call" | custom-call | tf_op jit(solution)/shard_map/weight_grad/pallas_call | solution.py:923
  (13 shorter events, 0.0 us)
Async XLA Ops:
  0.6 1.0 %copy-start.2 = (bf16[512,256]{1,0:T(8,128)(2,1)S(1)}, bf16[512,256]{1,0:T(8,128)(2,1)}, u32[]{:S(2)}) copy-start(bf16[512,256]{1,0:T(8,128)(2,1)} %constant.25.clone.x_in) | copy-start | bytes 786436
  1.6 1.0 %copy-start.5 = (bf16[1024,256]{1,0:T(8,128)(2,1)S(1)}, bf16[1024,256]{1,0:T(8,128)(2,1)}, u32[]{:S(2)}) copy-start(bf16[1024,256]{1,0:T(8,128)(2,1)} %constant.20.clone.z_in) | copy-start | bytes 1572868
  2.6 0.9 %copy-start.10 = (bf16[512,256]{1,0:T(8,128)(2,1)S(1)}, bf16[512,256]{1,0:T(8,128)(2,1)}, u32[]{:S(2)}) copy-start(bf16[512,256]{1,0:T(8,128)(2,1)} %constant.27.clone.x_out) | copy-start | bytes 786436
  3.6 0.8 copy-start.11
  4.4 0.7 copy-start.14
  5.1 29.0 %copy-start = (bf16[64,2,64,128]{3,2,1,0:T(8,128)(2,1)S(1)}, bf16[64,2,64,128]{3,2,1,0:T(8,128)(2,1)}, u32[]{:S(2)}) copy-start(bf16[64,2,64,128]{3,2,1,0:T(8,128)(2,1)} %feat.1) | copy-start | bytes 6291460
  5.1 29.0 %copy-start.4 = (bf16[256,1024]{1,0:T(8,128)(2,1)S(1)}, bf16[256,1024]{1,0:T(8,128)(2,1)}, u32[]{:S(2)}) copy-start(bf16[256,1024]{1,0:T(8,128)(2,1)} %constant.21.clone.z_out) | copy-start | bytes 1572868
  5.1 29.0 %copy-start.6 = (bf16[1024,256]{1,0:T(8,128)(2,1)S(1)}, bf16[1024,256]{1,0:T(8,128)(2,1)}, u32[]{:S(2)}) copy-start(bf16[1024,256]{1,0:T(8,128)(2,1)} %constant.20.clone.z_in) | copy-start | bytes 1572868
  5.1 29.0 %copy-start.9 = (bf16[512,256]{1,0:T(8,128)(2,1)S(1)}, bf16[512,256]{1,0:T(8,128)(2,1)}, u32[]{:S(2)}) copy-start(bf16[512,256]{1,0:T(8,128)(2,1)} %constant.29.clone.y_out) | copy-start | bytes 786436
  5.1 29.0 %copy-start.12 = (bf16[128,256]{1,0:T(8,128)(2,1)S(1)}, bf16[128,256]{1,0:T(8,128)(2,1)}, u32[]{:S(2)}) copy-start(bf16[128,256]{1,0:T(8,128)(2,1)} %constant.22.clone.y_in) | copy-start | bytes 196612
  5.2 29.0 %copy-start.15 = (f32[64]{0:T(128)S(1)}, f32[64]{0:T(128)}, u32[]{:S(2)}) copy-start(f32[64]{0:T(128)} %bias.1) | copy-start | bytes 772
  32.8 1.3 %copy-start.7 = (bf16[1024,1024]{1,0:T(8,128)(2,1)}, bf16[1024,1024]{1,0:T(8,128)(2,1)S(1)}, u32[]{:S(2)}) copy-start(bf16[1024,1024]{1,0:T(8,128)(2,1)S(1)} %get-tuple-element.13.kron) | copy-start | bytes 6291460
  34.1 15.6 %copy-start.3 = (bf16[512,256]{1,0:T(8,128)(2,1)S(1)}, bf16[512,256]{1,0:T(8,128)(2,1)}, u32[]{:S(2)}) copy-start(bf16[512,256]{1,0:T(8,128)(2,1)} %constant.25.clone.x_in) | copy-start | bytes 786436
  34.1 15.6 %copy-start.8 = (bf16[512,256]{1,0:T(8,128)(2,1)S(1)}, bf16[512,256]{1,0:T(8,128)(2,1)}, u32[]{:S(2)}) copy-start(bf16[512,256]{1,0:T(8,128)(2,1)} %constant.26.clone.x_turn) | copy-start | bytes 786436
  34.1 15.6 %copy-start.13 = (bf16[128,256]{1,0:T(8,128)(2,1)S(1)}, bf16[128,256]{1,0:T(8,128)(2,1)}, u32[]{:S(2)}) copy-start(bf16[128,256]{1,0:T(8,128)(2,1)} %constant.28.clone.x_back) | copy-start | bytes 196612
  49.8 22.4 %copy-start.1 = (bf16[1024,1024]{1,0:T(8,128)(2,1)S(1)}, bf16[1024,1024]{1,0:T(8,128)(2,1)}, u32[]{:S(2)}) copy-start(bf16[1024,1024]{1,0:T(8,128)(2,1)} %constant.24.clone.unorder) | copy-start | bytes 6291460

commit v2 on v0

--- a/solution.py
+++ b/solution.py
@@ -3,6 +3,7 @@
 
 import jax
 import jax.numpy as jnp
+import numpy as np
 from jax import lax
 from jax.experimental import pallas as pl
 from jax.experimental.pallas import tpu as pltpu
@@ -170,7 +171,7 @@
     )(upstream, depth_grad, weight_back, depth_basis)
 
 
-def body(features, cotangent, spectral_weight, channel_weight, channel_bias):
+def plain_body(features, cotangent, spectral_weight, channel_weight, channel_bias):
     channels, planes, lines, depth_len = features.shape
     devices = lax.axis_size("gx")
     all_planes = planes * devices
@@ -273,6 +274,668 @@
     return (activated, feature_grad, spectral_grad)
 
 
+MESH = pl.DeviceIdType.MESH
+F32 = jnp.float32
+BF16 = jnp.bfloat16
+MB = 1024 * 1024
+
+
+def host_cos_sin(wavenum, length):
+    angles = (np.outer(wavenum, np.arange(length)) % length).astype(np.float32) * np.float32(
+        2.0 * math.pi / length
+    )
+    return np.cos(angles), np.sin(angles)
+
+
+def host_freq(retained, length):
+    ladder = np.arange(retained)
+    return np.where(ladder < retained // 2, ladder, length - retained + ladder)
+
+
+def host_minus(retained, length):
+    cosine, sine = host_cos_sin(host_freq(retained, length), length)
+    cosine, sine = cosine.T, sine.T
+    return np.stack([np.stack([cosine, -sine], 1), np.stack([sine, cosine], 1)], 1)
+
+
+def host_plus(retained, length):
+    cosine, sine = host_cos_sin(host_freq(retained, length), length)
+    return np.stack([np.stack([cosine, sine], 1), np.stack([-sine, cosine], 1)], 1)
+
+
+def host_tables(devices, lines, depth_len, channels):
+    all_planes = 2 * devices
+    two = np.eye(2)
+    eight = np.eye(8)
+    cosine, sine = host_cos_sin(np.arange(MZ), depth_len)
+    depth = np.stack([cosine, -sine], 0)
+    z_in = np.einsum("akz,cd->czakd", depth, eight).reshape(8 * depth_len, 16 * MZ)
+    minus_y = host_minus(MY, lines).reshape(lines, 2, 2, devices, 2)
+    y_in = np.einsum("yabdk,xw->dkbwxay", minus_y, two).reshape(8 * devices, 4 * lines)
+    groups = channels // 8
+    source = np.arange(MZ * channels).reshape(groups, MZ, 8)
+    target = source.transpose(1, 0, 2).reshape(-1)
+    order = np.zeros((MZ * channels, MZ * channels))
+    order[target, np.arange(MZ * channels)] = 1.0
+    minus_x = host_minus(MX, all_planes).reshape(devices, 2, 2, 2, MX)
+    x_in = np.einsum("sxabk,hg,jl,p->hkjpbsglax", minus_x, two, two, np.ones(2)).reshape(
+        16 * MX, 16 * devices
+    )
+    swapped = np.stack([minus_x[:, :, :, 1], -minus_x[:, :, :, 0]], 3)
+    x_turn = np.einsum("sxabk,hg,jl,p->hkjpbsglax", swapped, two, two, np.ones(2)).reshape(
+        16 * MX, 16 * devices
+    )
+    plus_x = host_plus(MX, all_planes).reshape(MX, 2, 2, devices, 2)
+    crossed = np.stack([-plus_x[:, :, 1], plus_x[:, :, 0]], 2)
+    both = np.stack([plus_x, crossed], 0)
+    x_out = np.einsum("rkabsx,pq,jl->prsjbxklqa", both, two, two).reshape(32 * devices, 8 * MX)
+    x_back = np.einsum("kabsx,jl,q->sjbxklqa", plus_x, two, np.ones(2)).reshape(
+        8 * devices, 8 * MX
+    )
+    plus_y = host_plus(MY, lines).reshape(devices, 2, 2, 2, lines)
+    y_out = np.einsum("skaby,hg,xw->xbhysgkaw", plus_y, two, two).reshape(8 * lines, 16 * devices)
+    tables = dict(
+        z_in=z_in, z_out=z_in.T, y_in=y_in, order=order, unorder=order.T, x_in=x_in,
+        x_turn=x_turn, x_out=x_out, x_back=x_back, y_out=y_out,
+    )
+    return {name: jnp.asarray(np.ascontiguousarray(t), BF16) for name, t in tables.items()}
+
+
+def fdot(left, right):
+    return jnp.dot(left, right, preferred_element_type=F32)
+
+
+def greet(devices):
+    me, group = lax.axis_index("gx"), lax.axis_index("grp")
+    barrier = pltpu.get_barrier_semaphore()
+
+    @pl.loop(1, devices)
+    def _(step):
+        pl.semaphore_signal(
+            barrier, inc=1, device_id=(group, lax.rem(me + step, devices)), device_id_type=MESH
+        )
+
+    def arrived():
+        pl.semaphore_wait(barrier, devices - 1)
+
+    return arrived
+
+
+def swap_start(devices, sent, got, send_sem, recv_sem, stage):
+    me, group = lax.axis_index("gx"), lax.axis_index("grp")
+
+    def copy(step):
+        target = lax.rem(me + step, devices)
+        return pltpu.make_async_remote_copy(
+            src_ref=sent.at[target],
+            dst_ref=got.at[me],
+            send_sem=send_sem.at[stage, step],
+            recv_sem=recv_sem.at[stage, step],
+            device_id=(group, target),
+            device_id_type=MESH,
+        )
+
+    @pl.loop(1, devices)
+    def _(step):
+        copy(step).start()
+
+    got[me] = sent[me]
+
+    def finish():
+        @pl.loop(1, devices)
+        def _(step):
+            copy(step).wait_recv()
+
+    def drained():
+        @pl.loop(1, devices)
+        def _(step):
+            copy(step).wait_send()
+
+    return finish, drained
+
+
+def to_chunks(devices, lines_ref, y_in, order, sent):
+    rows = fdot(y_in[...], lines_ref[...]).astype(BF16)
+    rows = fdot(rows, order[...])
+    lanes = rows.shape[1]
+    halves = [
+        rows[:, h * lanes // 2 : (h + 1) * lanes // 2].reshape(devices, 8, lanes // 2)
+        for h in range(2)
+    ]
+    chunk = jnp.concatenate(halves, 1).astype(BF16)
+    for u in range(2):
+        sent[u] = chunk[:, :, u * lanes // 4 : (u + 1) * lanes // 4]
+
+
+def mode_block(weights, k_pair, half, pair):
+    def one(kx):
+        return jnp.concatenate(
+            [weights[k2, half * 8 + pair * 2 + parity, kx] for k2 in range(2) for parity in range(2)],
+            0,
+        )
+
+    return jnp.concatenate([one(2 * k_pair), one(2 * k_pair + 1)], 1)
+
+
+def iotas():
+    row = lax.broadcasted_iota(jnp.int32, (8, 128), 0)
+    lane = lax.broadcasted_iota(jnp.int32, (8, 128), 1)
+    return row, lane
+
+
+def weight_copies(weights_hbm, weights, sem):
+    def copy(half, pair):
+        kz = pl.ds(half * 8 + pair * 2, 2)
+        return pltpu.make_async_copy(
+            weights_hbm.at[:, kz], weights.at[:, kz], sem.at[half, pair]
+        )
+
+    return copy
+
+
+def fill_kron(channel_weight, out, contract):
+    size = out.shape[0]
+    channels = channel_weight.shape[0]
+
+    def spread(rows, first, axis):
+        shape = (rows, channels) if axis == 0 else (channels, rows)
+        long = lax.broadcasted_iota(jnp.int32, shape, axis)
+        short = lax.broadcasted_iota(jnp.int32, shape, 1 - axis)
+        return jnp.where(long // 16 + first == short, 1.0, 0.0).astype(BF16)
+
+    columns = spread(size, 0, 1)
+    line = lax.broadcasted_iota(jnp.int32, (128, size), 0) % 16
+    same = line == lax.broadcasted_iota(jnp.int32, (128, size), 1) % 16
+
+    @pl.loop(0, size // 128)
+    def _(block):
+        rows = lax.dot_general(
+            spread(128, block * 8, 0),
+            channel_weight[...],
+            (((1,), (1 - contract,)), ((), ())),
+            preferred_element_type=F32,
+        ).astype(BF16)
+        out[pl.ds(pl.multiple_of(block * 128, 128), 128), :] = jnp.where(
+            same, fdot(rows, columns), 0.0
+        ).astype(BF16)
+
+
+TABLES = (
+    "z_in", "y_in", "order", "x_in", "x_out", "y_out", "unorder", "z_out", "x_turn", "x_back",
+)
+EARLY = 3
+
+
+def layer_kernel(
+    devices, forward_scale, inverse_scale,
+    feat_hbm, cot_hbm, weights_hbm, channel_weight, bias, *refs,
+):
+    number = len(TABLES)
+    tables_hbm = dict(zip(TABLES, refs[:number]))
+    act, grad, lefts, pairs = refs[number : number + 4]
+    tables = dict(zip(TABLES, refs[number + 4 : 2 * number + 4]))
+    (
+        feat, cot, weights, kron, kron_back, pointwise, lines_part, blocks, spectral,
+        up_wide, sent, got, coeffs, modes, turned, mixed,
+        feat_sem, load_sem, weight_sem, send_sem, recv_sem,
+    ) = refs[2 * number + 4 :]
+    channels, planes, lines, depth_len = feat.shape
+    groups = channels // 8
+    rows = 16
+    arrived = greet(devices)
+    pieces = feat_sem.shape[0]
+    share = channels // pieces
+
+    def load_feat(piece):
+        here = pl.ds(piece * share, share)
+        return pltpu.make_async_copy(feat_hbm.at[here], feat.at[here], feat_sem.at[piece])
+
+    loads = {
+        name: pltpu.make_async_copy(tables_hbm[name], tables[name], load_sem.at[i])
+        for i, name in enumerate(TABLES)
+    }
+    load_cot = pltpu.make_async_copy(cot_hbm, cot, load_sem.at[number])
+    loads["z_in"].start()
+    for piece in range(pieces):
+        load_feat(piece).start()
+    for name in TABLES[1:EARLY]:
+        loads[name].start()
+    weight_copy = weight_copies(weights_hbm, weights, weight_sem)
+    loads["z_in"].wait()
+
+    @pl.loop(0, pieces)
+    def _(piece):
+        load_feat(piece).wait()
+        for local in range(share // 8):
+            group = piece * (share // 8) + local
+            for plane in range(planes):
+                wide = jnp.concatenate([feat[group * 8 + i, plane] for i in range(8)], 1)
+                part = fdot(wide, tables["z_in"][...]).astype(BF16)
+                for a in range(2):
+                    lines_part[
+                        pl.ds((plane * 2 + a) * lines, lines),
+                        pl.ds(pl.multiple_of(group * 128, 128), 128),
+                    ] = part[:, a * 128 : (a + 1) * 128]
+
+    loads["x_in"].start()
+    for pair in range(2):
+        for half in range(2):
+            weight_copy(half, pair).start()
+    for name in TABLES[EARLY + 1 :]:
+        loads[name].start()
+    for pair in range(2, 4):
+        for half in range(2):
+            weight_copy(half, pair).start()
+    load_cot.start()
+    for name in TABLES[1:EARLY]:
+        loads[name].wait()
+    to_chunks(devices, lines_part, tables["y_in"], tables["order"], sent.at[0])
+    arrived()
+
+    def swap(stage, u):
+        return swap_start(
+            devices, sent.at[stage, u], got.at[stage, u], send_sem, recv_sem, 2 * stage + u
+        )
+
+    ends = [swap(0, u) for u in range(2)]
+
+    def point(block):
+        here = pl.ds(pl.multiple_of(block * rows, rows), rows)
+        both = jnp.concatenate(
+            [feat[:, x, here].reshape(channels * rows, depth_len) for x in range(planes)], 1
+        )
+        pointwise[block] = fdot(kron[...], both)
+
+    fill_kron(channel_weight, kron, 1)
+
+    @pl.loop(0, 2)
+    def _(block):
+        point(block)
+
+    for name in TABLES[EARLY:]:
+        loads[name].wait()
+    row, lane = iotas()
+    own = [(row // 2) == (lane // 64 + 2 * k2) for k2 in range(2)]
+    low_tall = lax.broadcasted_iota(jnp.int32, (8 * devices, 128), 1) < 64
+    low = lane < 64
+    direct = low == ((row // 2) % 2 == 0)
+    first_line = row < 4
+    zero = jnp.zeros((8, 128), F32)
+
+    for u in range(2):
+        ends[u][0]()
+        source = got[0, u].reshape(16 * devices, 256)
+        coeffs[u] = (fdot(tables["x_in"][...], source) * forward_scale).reshape(2, MX, 8, 256)
+
+        @pl.loop(0, 4)
+        def _(part):
+            half, local = part // 2, part % 2
+            weight_copy(half, 2 * u + local).wait()
+            span = pl.ds(pl.multiple_of(local * 128, 128), 128)
+
+            def step(k_pair, carry):
+                left = []
+                for i in range(2):
+                    block = coeffs[u, half, 2 * k_pair + i, :, span]
+                    left.append(
+                        jnp.concatenate([jnp.where(own[k2], block, 0.0) for k2 in range(2)], 1)
+                    )
+                left = jnp.concatenate(left, 0).astype(BF16)
+                out = fdot(left, mode_block(weights, k_pair, half, 2 * u + local))
+                out = jnp.concatenate([out[:8, :128], out[8:, 128:]], 0).astype(BF16)
+                mixed[half, pl.ds(pl.multiple_of(k_pair * 16, 16), 16), span] = out
+                return carry
+
+            lax.fori_loop(0, MX // 2, step, 0, unroll=8)
+
+        halves = []
+        for half in range(2):
+            every = fdot(tables["x_out"][...], mixed[half])
+            size = 8 * devices
+            tiles = []
+            for local in range(2):
+                even, even_x, odd, odd_x = [
+                    every[i * size : (i + 1) * size, local * 128 : (local + 1) * 128]
+                    for i in range(4)
+                ]
+                tiles.append(
+                    jnp.where(low_tall, even, odd_x)
+                    + pltpu.roll(jnp.where(low_tall, odd, even_x), 64, 1)
+                )
+            halves.append(jnp.concatenate(tiles, 1).reshape(devices, 8, 256))
+        sent[1, u] = jnp.concatenate(halves, 1).astype(BF16)
+        ends.append(swap(1, u))
+
+    @pl.loop(2, lines // rows)
+    def _(block):
+        point(block)
+
+    fill_kron(channel_weight, kron_back, 0)
+
+    @pl.loop(0, 2)
+    def _(k_half):
+        here = pl.ds(k_half * (MX // 2), MX // 2)
+        for index in range(8):
+            half, u, local = index // 4, (index % 4) // 2, index % 2
+            values = coeffs[u, half, here, :, local * 128 : (local + 1) * 128]
+            wide = jnp.concatenate(
+                [jnp.where(own[k2][None], values, 0.0).reshape(128, 128) for k2 in range(2)], 1
+            )
+            lefts[index, k_half] = wide.T.astype(BF16)
+
+    load_cot.wait()
+    ends[2][0]()
+    ends[3][0]()
+    to_lines(devices, got.at[1], tables["y_out"], tables["unorder"], blocks)
+
+    @pl.loop(0, lines // rows)
+    def _(block):
+        line = pl.ds(pl.multiple_of(block * rows, rows), rows)
+        spectral[...] = fdot(blocks[block], tables["z_out"][...])
+
+        @pl.loop(0, groups)
+        def _(group):
+            for plane in range(planes):
+                here = pl.ds(pl.multiple_of((plane * groups + group) * rows, rows), rows)
+                for i in range(8):
+                    o = group * 8 + i
+                    hidden = (
+                        spectral[here, i * 128 : (i + 1) * 128] * inverse_scale
+                        + pointwise[
+                            block,
+                            pl.ds(pl.multiple_of(o * rows, rows), rows),
+                            plane * 128 : (plane + 1) * 128,
+                        ]
+                        + bias[o]
+                    )
+                    activated, derivative = gelu_parts(hidden)
+                    act[o, plane, line] = activated.astype(BF16)
+                    up_wide[block, here, i * 128 : (i + 1) * 128] = (
+                        cot[o, plane, line].astype(F32) * derivative
+                    ).astype(BF16)
+
+        part = (fdot(up_wide[block], tables["z_in"][...]) * inverse_scale).astype(BF16)
+        for plane in range(planes):
+            for a in range(2):
+                for group in range(groups):
+                    first = (plane * groups + group) * rows
+                    lines_part[
+                        pl.ds(
+                            pl.multiple_of((plane * 2 + a) * lines + block * rows, rows), rows
+                        ),
+                        group * 128 : (group + 1) * 128,
+                    ] = part[first : first + rows, a * 128 : (a + 1) * 128]
+
+    to_chunks(devices, lines_part, tables["y_in"], tables["order"], sent.at[2])
+    ends += [swap(2, u) for u in range(2)]
+
+    @pl.loop(0, lines // rows)
+    def _(block):
+        both = []
+        for plane in range(planes):
+            tiles = []
+            for o in range(channels):
+                first = (plane * groups + o // 8) * rows
+                tiles.append(
+                    up_wide[block, first : first + rows, (o % 8) * 128 : (o % 8 + 1) * 128]
+                )
+            both.append(jnp.concatenate(tiles, 0))
+        pointwise[block] = fdot(kron_back[...], jnp.concatenate(both, 1))
+
+    for u in range(2):
+        ends[4 + u][0]()
+        source = got[2, u].reshape(16 * devices, 256)
+        modes[...] = fdot(tables["x_in"][...], source).reshape(2, MX, 8, 256)
+        turned[...] = fdot(tables["x_turn"][...], source).reshape(2, MX, 8, 256)
+
+        @pl.loop(0, 4)
+        def _(part):
+            half, local = part // 2, part % 2
+            span = pl.ds(pl.multiple_of(local * 128, 128), 128)
+
+            def step(k_pair, carry):
+                here = pl.ds(pl.multiple_of(k_pair * 16, 16), 16)
+                tiles = [
+                    pair_tile(
+                        modes[half, 2 * k_pair + i, :, span],
+                        turned[half, 2 * k_pair + i, :, span],
+                        low,
+                        direct,
+                    )
+                    for i in range(2)
+                ]
+                pairs[half * 4 + 2 * u + local, here] = jnp.concatenate(tiles, 0).astype(BF16)
+                left = jnp.concatenate(
+                    [jnp.concatenate([tiles[0], zero], 1), jnp.concatenate([zero, tiles[1]], 1)], 0
+                ).astype(BF16)
+                out = lax.dot_general(
+                    left,
+                    mode_block(weights, k_pair, half, 2 * u + local),
+                    (((1,), (1,)), ((), ())),
+                    preferred_element_type=F32,
+                )
+                kept = []
+                for i in range(2):
+                    here_rows = out[8 * i : 8 * i + 8]
+                    kept.append(
+                        jnp.where(
+                            direct,
+                            jnp.where(first_line, here_rows[:, :128], here_rows[:, 128:]),
+                            0.0,
+                        )
+                    )
+                mixed[half, here, span] = (jnp.concatenate(kept, 0) * forward_scale).astype(BF16)
+                return carry
+
+            lax.fori_loop(0, MX // 2, step, 0, unroll=8)
+
+        sent[3, u] = jnp.concatenate(
+            [fdot(tables["x_back"][...], mixed[half]).reshape(devices, 8, 256) for half in range(2)],
+            1,
+        ).astype(BF16)
+        ends.append(swap(3, u))
+
+    ends[6][0]()
+    ends[7][0]()
+    to_lines(devices, got.at[3], tables["y_out"], tables["unorder"], blocks)
+
+    @pl.loop(0, lines // rows)
+    def _(block):
+        line = pl.ds(pl.multiple_of(block * rows, rows), rows)
+        spectral[...] = fdot(blocks[block], tables["z_out"][...])
+
+        @pl.loop(0, groups)
+        def _(group):
+            for plane in range(planes):
+                here = pl.ds(pl.multiple_of((plane * groups + group) * rows, rows), rows)
+                for i in range(8):
+                    o = group * 8 + i
+                    total = (
+                        spectral[here, i * 128 : (i + 1) * 128]
+                        + pointwise[
+                            block,
+                            pl.ds(pl.multiple_of(o * rows, rows), rows),
+                            plane * 128 : (plane + 1) * 128,
+                        ]
+                    )
+                    grad[o, plane, line] = total.astype(BF16)
+
+    for end in ends:
+        end[1]()
+
+
+def to_lines(devices, back, y_out, unorder, blocks):
+    lines_u = [fdot(y_out[...], back[u].reshape(16 * devices, 256)).astype(BF16) for u in range(2)]
+    lines = lines_u[0].shape[0] // 8
+    for plane in range(2):
+        for part in range(2):
+            pieces = []
+            for half in range(2):
+                first = ((plane * 2 + part) * 2 + half) * lines
+                pieces += [lines_u[u][first : first + lines] for u in range(2)]
+            rows = fdot(jnp.concatenate(pieces, 1), unorder[...]).astype(BF16)
+            groups = rows.shape[1] // 128
+            for block in range(lines // 16):
+                for group in range(groups):
+                    blocks[
+                        block,
+                        (plane * groups + group) * 16 : (plane * groups + group + 1) * 16,
+                        part * 128 : (part + 1) * 128,
+                    ] = rows[block * 16 : (block + 1) * 16, group * 128 : (group + 1) * 128]
+
+
+def pair_tile(straight, other, low, direct):
+    return jnp.where(
+        direct,
+        jnp.where(low, straight, other),
+        pltpu.roll(jnp.where(low, other, straight), 64, 1),
+    )
+
+
+def weight_grad_kernel(
+    weight_scale, act_in, grad_in, lefts, pairs, act_out, grad_out, out_hbm, buffer, sem, field_sem,
+):
+    fields = [
+        pltpu.make_async_copy(act_in, act_out, field_sem.at[0]),
+        pltpu.make_async_copy(grad_in, grad_out, field_sem.at[1]),
+    ]
+    for copy in fields:
+        copy.start()
+    block = lax.broadcasted_iota(jnp.int32, (128, 256), 0) // 8
+    side = lax.broadcasted_iota(jnp.int32, (128, 256), 1) // 128
+
+    def copy(index, slot):
+        return pltpu.make_async_copy(
+            buffer.at[slot], out_hbm.at[:, pl.ds(2 * index, 2)], sem.at[slot]
+        )
+
+    @pl.loop(0, 8)
+    def _(index):
+        slot = lax.rem(index, 2)
+
+        @pl.when(index >= 2)
+        def _():
+            copy(index - 2, slot).wait()
+
+        @pl.loop(0, 2)
+        def _(k_half):
+            here = pl.ds(pl.multiple_of(k_half * 128, 128), 128)
+            right = pairs[index, here].astype(F32) * weight_scale
+            right = jnp.concatenate([right, right], 1)
+            for i in range(MX // 4):
+                kept = jnp.where(block == 2 * i + side, right, 0.0).astype(BF16)
+                out = fdot(lefts[index, k_half], kept).astype(BF16)
+                for s in range(2):
+                    for k2 in range(2):
+                        for parity in range(2):
+                            first = (k2 * 2 + parity) * 64
+                            buffer[slot, k2, parity, k_half * (MX // 2) + 2 * i + s] = out[
+                                first : first + 64, s * 128 : (s + 1) * 128
+                            ]
+
+        copy(index, slot).start()
+
+    copy(6, 0).wait()
+    copy(7, 1).wait()
+    for one in fields:
+        one.wait()
+
+
+def vmem(*shape, dtype=BF16):
+    return pltpu.VMEM(shape, dtype)
+
+
+WHOLE = pl.BlockSpec(memory_space=pltpu.VMEM)
+ANYWHERE = pl.BlockSpec(memory_space=pl.ANY)
+
+
+def block_body(features, cotangent, spectral_weight, channel_weight, channel_bias):
+    channels, planes, lines, depth_len = features.shape
+    devices = lax.axis_size("gx")
+    all_planes = planes * devices
+    number = MX * MY * MZ
+    forward_scale = 1.0 / math.sqrt(all_planes * lines * depth_len)
+    inverse_scale = 1.0 / math.sqrt(number)
+    weight_scale = math.sqrt(number / (all_planes * lines * depth_len))
+    tables = host_tables(devices, lines, depth_len, channels)
+    tables = [tables[name] for name in TABLES]
+    weights = spectral_weight.reshape(2, MZ, MX, channels, 2 * channels)
+    wide = MZ * channels
+    rows = 16
+    steps = lines // rows
+    dma = pltpu.SemaphoreType.DMA
+    like = jax.ShapeDtypeStruct(features.shape, BF16)
+    lefts = (8, 2, 256, 128)
+    pairs = (8, 8 * MX, 128)
+    activated, feature_grad, left, pair = pl.pallas_call(
+        functools.partial(layer_kernel, devices, forward_scale, inverse_scale),
+        out_shape=[
+            vmem(*features.shape), vmem(*features.shape), vmem(*lefts), vmem(*pairs)
+        ],
+        in_specs=[ANYWHERE] * 3
+        + [WHOLE, pl.BlockSpec(memory_space=pltpu.SMEM)]
+        + [ANYWHERE] * len(tables),
+        out_specs=[WHOLE] * 4,
+        scratch_shapes=[vmem(*table.shape) for table in tables]
+        + [
+            vmem(*features.shape),
+            vmem(*features.shape),
+            vmem(*weights.shape),
+            vmem(channels * rows, channels * rows),
+            vmem(channels * rows, channels * rows),
+            vmem(steps, channels * rows, planes * depth_len, dtype=F32),
+            vmem(4 * lines, wide),
+            vmem(steps, 2 * wide // 8, 256),
+            vmem(planes * channels * 2, 8 * depth_len, dtype=F32),
+            vmem(steps, planes * channels * 2, 8 * depth_len),
+            vmem(4, 2, devices, 16, 256),
+            vmem(4, 2, devices, 16, 256),
+            vmem(2, 2, MX, 8, 256, dtype=F32),
+            vmem(2, MX, 8, 256, dtype=F32),
+            vmem(2, MX, 8, 256, dtype=F32),
+            vmem(2, 8 * MX, 256),
+            dma((4,)),
+            dma((len(tables) + 1,)),
+            dma((2, 4)),
+            dma((8, devices)),
+            dma((8, devices)),
+        ],
+        compiler_params=pltpu.CompilerParams(
+            collective_id=0, has_side_effects=True, vmem_limit_bytes=56 * MB
+        ),
+        name="layer",
+    )(features, cotangent, weights, channel_weight, channel_bias, *tables)
+    activated, feature_grad, spectral_grad = pl.pallas_call(
+        functools.partial(weight_grad_kernel, weight_scale),
+        out_shape=[like, like, jax.ShapeDtypeStruct(weights.shape, BF16)],
+        in_specs=[WHOLE] * 4,
+        out_specs=[ANYWHERE] * 3,
+        scratch_shapes=[
+            vmem(2, 2, 2, MX, channels, 2 * channels),
+            dma((2,)),
+            dma((2,)),
+        ],
+        compiler_params=pltpu.CompilerParams(vmem_limit_bytes=40 * MB),
+        name="weight_grad",
+    )(activated, feature_grad, left, pair)
+    return (activated, feature_grad, spectral_grad.reshape(spectral_weight.shape))
+
+
+def body(features, cotangent, spectral_weight, channel_weight, channel_bias):
+    channels, planes, lines, depth_len = features.shape
+    devices = lax.axis_size("gx")
+    fits = (
+        2 * devices == MY
+        and planes == 2
+        and channels == 64
+        and lines == 64
+        and depth_len == 128
+        and spectral_weight.shape[0] == 2 * MZ * MX
+    )
+    chosen = block_body if fits else plain_body
+    return chosen(features, cotangent, spectral_weight, channel_weight, channel_bias)
+
+
 def solution(mesh):
     in_specs = (
         P("grp", "gx", None, None),

time: 123 us -> 70.4 us (0.57)
  Pallas kernels: 15.4 us -> 69.5 us
  matrix products: 38.1 us -> 0 us
  waiting for transfers between devices: 28.1 us -> 0 us
  starting transfers between devices: 18.4 us -> 0 us
  local copies, waits for them, and re-layouts: 17.1 us -> 0 us
  other arithmetic: 4.03 us -> 0 us
    pallas_call x2, Pallas kernels: 15.4 us -> 69.5 us  [the longest x1 59.4 us: block_body(): pl.pallas_call(functools.partial(layer_kernel, devices, forward_scale, in...]
    dot_general x12 -> x0, matrix products: 38.1 us -> none  [the longest x1 12.3 us: body(): jnp.einsum('mcj,mbj->mbc', spectral_weight, pairs, preferred_element_type...]
    all_to_all x4 -> x0, waiting for transfers between devices: 28.1 us -> none  [exchange(): return lax.all_to_all(blocks, 'gx', 0, 0, tiled=True)]
    all_to_all x4 -> x0, starting transfers between devices: 18.4 us -> none  [exchange(): return lax.all_to_all(blocks, 'gx', 0, 0, tiled=True)]
    reshape x12 -> x0, local copies, waits for them, and re-layouts: 7.79 us -> none  [the longest x2 1.91 us: to_planes(): blocks = rows.reshape(devices, planes * owned_pairs, wide)]
    convert_element_type x7 -> x0, local copies, waits for them, and re-layouts: 4.06 us -> none  [the longest x1 0.68 us: body(): lines_back = jnp.einsum('xkzao,kaby->xyobz', planes_here, back_y, preferr...]
    another operation x12 -> x0, other arithmetic: 3.38 us -> none
    pallas_call x1 -> x0, local copies, waits for them, and re-layouts: 2.01 us -> none  [middle(): pl.pallas_call(functools.partial(middle_kernel, scale), grid=(planes, lin...]
  transfers between devices with their start and end apart: 4 -> 0, of which waited for: 4 -> 0; matrix products, arithmetic and copies ran while one was open for 9% -> 0% of each run, Pallas kernels for 0% -> 0%
where the time goes in v2:
time: 70.4 us; the launch traced here: 70.2 us
  Pallas kernels  69.5 us (99%)
    pallas_call x1, Pallas kernels, block_body(): pl.pallas_call(functools.partial(layer_kernel, devices, forward_scale, in...  59.4 us
    pallas_call x1, Pallas kernels, block_body(): pl.pallas_call(functools.partial(weight_grad_kernel, weight_scale), out_s...  10.1 us

profile of v2, /device:TPU:0, one launch (start us, length us, event | category | flops | bytes accessed | tf_op | source)
XLA Modules:
  0.0 70.2 jit_solution(9590693353264535184)
XLA Ops:
  0.6 59.4 %layer.1 = (bf16[64,2,64,128]{3,2,1,0:T(8,128)(2,1)S(1)}, bf16[64,2,64,128]{3,2,1,0:T(8,128)(2,1)S(1)}, bf16[8,2,256,128]{3,2,1,0:T(8,128)(2,1)S(1)}, bf16[8,256,128]{2,1,0:T(8,128)(2,1)S(1)}) custom-call(bf16[64,2,64,128]{3,2,1,0:T(8,128)(2,1)} %feat_hbm.1, bf16[64,2,64,128]{3,2,1,0:T(8,128)(2,1)} %cot_hbm.1, bf16[2,16,32,64,128]{4,3,2,1,0:T(8,128)(2,1)} %bitcast.2, ...), custom_call_target="tpu_custom_call" | custom-call | tf_op jit(solution)/shard_map/layer/pallas_call | solution.py:870
  60.1 10.1 %weight_grad.1 = (bf16[64,2,64,128]{3,2,1,0:T(8,128)(2,1)}, bf16[64,2,64,128]{3,2,1,0:T(8,128)(2,1)}, bf16[2,16,32,64,128]{4,3,2,1,0:T(8,128)(2,1)}) custom-call(bf16[64,2,64,128]{3,2,1,0:T(8,128)(2,1)S(1)} %get-tuple-element.10.act_in, bf16[64,2,64,128]{3,2,1,0:T(8,128)(2,1)S(1)} %get-tuple-element.11.grad_in, ...), custom_call_target="tpu_custom_call" | custom-call | tf_op jit(solution)/shard_map/weight_grad/pallas_call | solution.py:908

commit v3 on v2

--- a/solution.py
+++ b/solution.py
@@ -467,18 +467,18 @@
 
 
 def layer_kernel(
-    devices, forward_scale, inverse_scale,
+    devices, forward_scale, inverse_scale, weight_scale,
     feat_hbm, cot_hbm, weights_hbm, channel_weight, bias, *refs,
 ):
     number = len(TABLES)
     tables_hbm = dict(zip(TABLES, refs[:number]))
-    act, grad, lefts, pairs = refs[number : number + 4]
-    tables = dict(zip(TABLES, refs[number + 4 : 2 * number + 4]))
+    act, grad, weights, lefts, pairs = refs[number : number + 5]
+    tables = dict(zip(TABLES, refs[number + 5 : 2 * number + 5]))
     (
-        feat, cot, weights, kron, kron_back, pointwise, lines_part, blocks, spectral,
+        feat, cot, kron, kron_back, pointwise, lines_part, blocks, spectral,
         up_wide, sent, got, coeffs, modes, turned, mixed,
         feat_sem, load_sem, weight_sem, send_sem, recv_sem,
-    ) = refs[2 * number + 4 :]
+    ) = refs[2 * number + 5 :]
     channels, planes, lines, depth_len = feat.shape
     groups = channels // 8
     rows = 16
@@ -537,18 +537,28 @@
             devices, sent.at[stage, u], got.at[stage, u], send_sem, recv_sem, 2 * stage + u
         )
 
-    ends = [swap(0, u) for u in range(2)]
+    ends = [swap(0, 0)]
 
     def point(block):
         here = pl.ds(pl.multiple_of(block * rows, rows), rows)
         both = jnp.concatenate(
             [feat[:, x, here].reshape(channels * rows, depth_len) for x in range(planes)], 1
         )
-        pointwise[block] = fdot(kron[...], both)
+        total = fdot(kron[...], both)
+        for o in range(channels):
+            here = slice(o * rows, (o + 1) * rows)
+            pointwise[block, here] = total[here] + bias[o]
 
     fill_kron(channel_weight, kron, 1)
 
-    @pl.loop(0, 2)
+    @pl.loop(0, 1)
+    def _(block):
+        point(block)
+
+    ends[0][1]()
+    ends.append(swap(0, 1))
+
+    @pl.loop(1, 2)
     def _(block):
         point(block)
 
@@ -586,11 +596,11 @@
                 mixed[half, pl.ds(pl.multiple_of(k_pair * 16, 16), 16), span] = out
                 return carry
 
-            lax.fori_loop(0, MX // 2, step, 0, unroll=8)
+            lax.fori_loop(0, MX // 2, step, 0, unroll=16)
 
         halves = []
         for half in range(2):
-            every = fdot(tables["x_out"][...], mixed[half])
+            every = fdot(tables["x_out"][...], mixed[half]) * inverse_scale
             size = 8 * devices
             tiles = []
             for local in range(2):
@@ -633,20 +643,19 @@
         line = pl.ds(pl.multiple_of(block * rows, rows), rows)
         spectral[...] = fdot(blocks[block], tables["z_out"][...])
 
-        @pl.loop(0, groups)
+        @pl.loop(0, groups, unroll=True)
         def _(group):
             for plane in range(planes):
                 here = pl.ds(pl.multiple_of((plane * groups + group) * rows, rows), rows)
                 for i in range(8):
                     o = group * 8 + i
                     hidden = (
-                        spectral[here, i * 128 : (i + 1) * 128] * inverse_scale
+                        spectral[here, i * 128 : (i + 1) * 128]
                         + pointwise[
                             block,
                             pl.ds(pl.multiple_of(o * rows, rows), rows),
                             plane * 128 : (plane + 1) * 128,
                         ]
-                        + bias[o]
                     )
                     activated, derivative = gelu_parts(hidden)
                     act[o, plane, line] = activated.astype(BF16)
@@ -667,10 +676,9 @@
                     ] = part[first : first + rows, a * 128 : (a + 1) * 128]
 
     to_chunks(devices, lines_part, tables["y_in"], tables["order"], sent.at[2])
-    ends += [swap(2, u) for u in range(2)]
-
-    @pl.loop(0, lines // rows)
-    def _(block):
+    ends.append(swap(2, 0))
+
+    def point_back(block):
         both = []
         for plane in range(planes):
             tiles = []
@@ -681,6 +689,11 @@
                 )
             both.append(jnp.concatenate(tiles, 0))
         pointwise[block] = fdot(kron_back[...], jnp.concatenate(both, 1))
+
+    pl.loop(0, 3)(point_back)
+    ends[4][1]()
+    ends.append(swap(2, 1))
+    pl.loop(3, 4)(point_back)
 
     for u in range(2):
         ends[4 + u][0]()
@@ -727,7 +740,7 @@
                 mixed[half, here, span] = (jnp.concatenate(kept, 0) * forward_scale).astype(BF16)
                 return carry
 
-            lax.fori_loop(0, MX // 2, step, 0, unroll=8)
+            lax.fori_loop(0, MX // 2, step, 0, unroll=16)
 
         sent[3, u] = jnp.concatenate(
             [fdot(tables["x_back"][...], mixed[half]).reshape(devices, 8, 256) for half in range(2)],
@@ -735,6 +748,10 @@
         ).astype(BF16)
         ends.append(swap(3, u))
 
+    for index in (0, 1, 4, 5):
+        weight_grad_block(
+            weight_scale, lefts.at[index], pairs.at[index], weights.at[:, 2 * index : 2 * index + 2]
+        )
     ends[6][0]()
     ends[7][0]()
     to_lines(devices, got.at[3], tables["y_out"], tables["unorder"], blocks)
@@ -744,7 +761,7 @@
         line = pl.ds(pl.multiple_of(block * rows, rows), rows)
         spectral[...] = fdot(blocks[block], tables["z_out"][...])
 
-        @pl.loop(0, groups)
+        @pl.loop(0, groups, unroll=True)
         def _(group):
             for plane in range(planes):
                 here = pl.ds(pl.multiple_of((plane * groups + group) * rows, rows), rows)
@@ -760,7 +777,7 @@
                     )
                     grad[o, plane, line] = total.astype(BF16)
 
-    for end in ends:
+    for end in (ends[1], ends[2], ends[3], ends[5], ends[6], ends[7]):
         end[1]()
 
 
@@ -792,53 +809,53 @@
     )
 
 
+def weight_grad_block(weight_scale, left, pairs, out):
+    block = lax.broadcasted_iota(jnp.int32, (128, 256), 0) // 8
+    side = lax.broadcasted_iota(jnp.int32, (128, 256), 1) // 128
+
+    @pl.loop(0, 2)
+    def _(k_half):
+        here = pl.ds(pl.multiple_of(k_half * 128, 128), 128)
+        right = pairs[here].astype(F32) * weight_scale
+        right = jnp.concatenate([right, right], 1)
+        for i in range(MX // 4):
+            kept = jnp.where(block == 2 * i + side, right, 0.0).astype(BF16)
+            total = fdot(left[k_half], kept).astype(BF16)
+            for s in range(2):
+                for k2 in range(2):
+                    for parity in range(2):
+                        first = (k2 * 2 + parity) * 64
+                        out[k2, parity, k_half * (MX // 2) + 2 * i + s] = total[
+                            first : first + 64, s * 128 : (s + 1) * 128
+                        ]
+
+
 def weight_grad_kernel(
-    weight_scale, act_in, grad_in, lefts, pairs, act_out, grad_out, out_hbm, buffer, sem, field_sem,
+    weight_scale, act_in, grad_in, part_in, lefts, pairs, act_out, grad_out, out_hbm, buffer, sem,
+    field_sem,
 ):
-    fields = [
+    def place(index):
+        return out_hbm.at[:, 2 * index : 2 * index + 2]
+
+    copies = [
+        pltpu.make_async_copy(
+            part_in.at[:, 2 * index : 2 * index + 2], place(index), sem.at[index]
+        )
+        for index in (0, 1, 4, 5)
+    ]
+    copies += [
         pltpu.make_async_copy(act_in, act_out, field_sem.at[0]),
         pltpu.make_async_copy(grad_in, grad_out, field_sem.at[1]),
     ]
-    for copy in fields:
+    for copy in copies:
         copy.start()
-    block = lax.broadcasted_iota(jnp.int32, (128, 256), 0) // 8
-    side = lax.broadcasted_iota(jnp.int32, (128, 256), 1) // 128
-
-    def copy(index, slot):
-        return pltpu.make_async_copy(
-            buffer.at[slot], out_hbm.at[:, pl.ds(2 * index, 2)], sem.at[slot]
-        )
-
-    @pl.loop(0, 8)
-    def _(index):
-        slot = lax.rem(index, 2)
-
-        @pl.when(index >= 2)
-        def _():
-            copy(index - 2, slot).wait()
-
-        @pl.loop(0, 2)
-        def _(k_half):
-            here = pl.ds(pl.multiple_of(k_half * 128, 128), 128)
-            right = pairs[index, here].astype(F32) * weight_scale
-            right = jnp.concatenate([right, right], 1)
-            for i in range(MX // 4):
-                kept = jnp.where(block == 2 * i + side, right, 0.0).astype(BF16)
-                out = fdot(lefts[index, k_half], kept).astype(BF16)
-                for s in range(2):
-                    for k2 in range(2):
-                        for parity in range(2):
-                            first = (k2 * 2 + parity) * 64
-                            buffer[slot, k2, parity, k_half * (MX // 2) + 2 * i + s] = out[
-                                first : first + 64, s * 128 : (s + 1) * 128
-                            ]
-
-        copy(index, slot).start()
-
-    copy(6, 0).wait()
-    copy(7, 1).wait()
-    for one in fields:
-        one.wait()
+    for slot, index in enumerate((2, 3, 6, 7)):
+        weight_grad_block(weight_scale, lefts.at[index], pairs.at[index], buffer.at[slot])
+        copy = pltpu.make_async_copy(buffer.at[slot], place(index), sem.at[index])
+        copy.start()
+        copies.append(copy)
+    for copy in copies:
+        copy.wait()
 
 
 def vmem(*shape, dtype=BF16):
@@ -867,20 +884,20 @@
     like = jax.ShapeDtypeStruct(features.shape, BF16)
     lefts = (8, 2, 256, 128)
     pairs = (8, 8 * MX, 128)
-    activated, feature_grad, left, pair = pl.pallas_call(
-        functools.partial(layer_kernel, devices, forward_scale, inverse_scale),
+    activated, feature_grad, weight_part, left, pair = pl.pallas_call(
+        functools.partial(layer_kernel, devices, forward_scale, inverse_scale, weight_scale),
         out_shape=[
-            vmem(*features.shape), vmem(*features.shape), vmem(*lefts), vmem(*pairs)
+            vmem(*features.shape), vmem(*features.shape), vmem(*weights.shape), vmem(*lefts),
+            vmem(*pairs),
         ],
         in_specs=[ANYWHERE] * 3
         + [WHOLE, pl.BlockSpec(memory_space=pltpu.SMEM)]
         + [ANYWHERE] * len(tables),
-        out_specs=[WHOLE] * 4,
+        out_specs=[WHOLE] * 5,
         scratch_shapes=[vmem(*table.shape) for table in tables]
         + [
             vmem(*features.shape),
             vmem(*features.shape),
-            vmem(*weights.shape),
             vmem(channels * rows, channels * rows),
             vmem(channels * rows, channels * rows),
             vmem(steps, channels * rows, planes * depth_len, dtype=F32),
@@ -901,23 +918,23 @@
             dma((8, devices)),
         ],
         compiler_params=pltpu.CompilerParams(
-            collective_id=0, has_side_effects=True, vmem_limit_bytes=56 * MB
+            collective_id=0, has_side_effects=True, vmem_limit_bytes=40 * MB
         ),
         name="layer",
     )(features, cotangent, weights, channel_weight, channel_bias, *tables)
     activated, feature_grad, spectral_grad = pl.pallas_call(
         functools.partial(weight_grad_kernel, weight_scale),
         out_shape=[like, like, jax.ShapeDtypeStruct(weights.shape, BF16)],
-        in_specs=[WHOLE] * 4,
+        in_specs=[WHOLE] * 5,
         out_specs=[ANYWHERE] * 3,
         scratch_shapes=[
-            vmem(2, 2, 2, MX, channels, 2 * channels),
-            dma((2,)),
+            vmem(4, 2, 2, MX, channels, 2 * channels),
+            dma((8,)),
             dma((2,)),
         ],
-        compiler_params=pltpu.CompilerParams(vmem_limit_bytes=40 * MB),
+        compiler_params=pltpu.CompilerParams(vmem_limit_bytes=14 * MB),
         name="weight_grad",
-    )(activated, feature_grad, left, pair)
+    )(activated, feature_grad, weight_part, left, pair)
     return (activated, feature_grad, spectral_grad.reshape(spectral_weight.shape))
 
 

time: 70.4 us -> 61.6 us (0.88)
  Pallas kernels: 69.5 us -> 60.7 us
    pallas_call x1, Pallas kernels: 59.4 us -> 53.5 us  [block_body(): pl.pallas_call(functools.partial(layer_kernel, devices, forward_scale, in...]
    pallas_call x1, Pallas kernels: 10.1 us -> 7.2 us  [block_body(): pl.pallas_call(functools.partial(weight_grad_kernel, weight_scale), out_s...]
where the time goes in v3:
time: 61.6 us; the launch traced here: 61.4 us
  Pallas kernels  60.7 us (99%)
  between operations  0.64 us (1%)
    pallas_call x1, Pallas kernels, block_body(): pl.pallas_call(functools.partial(layer_kernel, devices, forward_scale, in...  53.5 us
    pallas_call x1, Pallas kernels, block_body(): pl.pallas_call(functools.partial(weight_grad_kernel, weight_scale), out_s...  7.2 us

profile of v3, /device:TPU:0, one launch (start us, length us, event | category | flops | bytes accessed | tf_op | source)
XLA Modules:
  0.0 61.4 jit_solution(15695195283258233569)
XLA Ops:
  0.6 53.5 %layer.1 = (bf16[64,2,64,128]{3,2,1,0:T(8,128)(2,1)S(1)}, bf16[64,2,64,128]{3,2,1,0:T(8,128)(2,1)S(1)}, bf16[2,16,32,64,128]{4,3,2,1,0:T(8,128)(2,1)S(1)}, bf16[...) custom-call(bf16[64,2,64,128]{3,2,1,0:T(8,128)(2,1)} %feat_hbm.1, bf16[64,2,64,128]{3,2,1,0:T(8,128)(2,1)} %cot_hbm.1, ...), custom_call_target="tpu_custom_call" | custom-call | tf_op jit(solution)/shard_map/layer/pallas_call | solution.py:887
  54.2 7.2 %weight_grad.1 = (bf16[64,2,64,128]{3,2,1,0:T(8,128)(2,1)}, bf16[64,2,64,128]{3,2,1,0:T(8,128)(2,1)}, bf16[2,16,32,64,128]{4,3,2,1,0:T(8,128)(2,1)}) custom-call(bf16[64,2,64,128]{3,2,1,0:T(8,128)(2,1)S(1)} %get-tuple-element.11.act_in, bf16[64,2,64,128]{3,2,1,0:T(8,128)(2,1)S(1)} %get-tuple-element.12.grad_in, ...), custom_call_target="tpu_custom_call" | custom-call | tf_op jit(solution)/shard_map/weight_grad/pallas_call | solution.py:925

commit v4 on v3

--- a/solution.py
+++ b/solution.py
@@ -464,6 +464,8 @@
     "z_in", "y_in", "order", "x_in", "x_out", "y_out", "unorder", "z_out", "x_turn", "x_back",
 )
 EARLY = 3
+LATE = 5
+PARTS = 2
 
 
 def layer_kernel(
@@ -506,16 +508,19 @@
     @pl.loop(0, pieces)
     def _(piece):
         load_feat(piece).wait()
-        for local in range(share // 8):
+        spots = [(local, plane) for local in range(share // 8) for plane in range(planes)]
+        wide = [
+            jnp.concatenate([feat[piece * share + local * 8 + i, plane] for i in range(8)], 1)
+            for local, plane in spots
+        ]
+        part = fdot(jnp.concatenate(wide, 0), tables["z_in"][...]).astype(BF16)
+        for spot, (local, plane) in enumerate(spots):
             group = piece * (share // 8) + local
-            for plane in range(planes):
-                wide = jnp.concatenate([feat[group * 8 + i, plane] for i in range(8)], 1)
-                part = fdot(wide, tables["z_in"][...]).astype(BF16)
-                for a in range(2):
-                    lines_part[
-                        pl.ds((plane * 2 + a) * lines, lines),
-                        pl.ds(pl.multiple_of(group * 128, 128), 128),
-                    ] = part[:, a * 128 : (a + 1) * 128]
+            for a in range(2):
+                lines_part[
+                    pl.ds((plane * 2 + a) * lines, lines),
+                    pl.ds(pl.multiple_of(group * 128, 128), 128),
+                ] = part[spot * lines : (spot + 1) * lines, a * 128 : (a + 1) * 128]
 
     loads["x_in"].start()
     for pair in range(2):
@@ -537,6 +542,12 @@
             devices, sent.at[stage, u], got.at[stage, u], send_sem, recv_sem, 2 * stage + u
         )
 
+    def lines_of(stage, arrivals):
+        for u in range(2):
+            arrivals[u][0]()
+            to_lines(u, got.at[stage], tables["y_out"], tables["unorder"], spectral.at[0])
+        to_blocks(spectral.at[0], blocks)
+
     ends = [swap(0, 0)]
 
     def point(block):
@@ -562,7 +573,7 @@
     def _(block):
         point(block)
 
-    for name in TABLES[EARLY:]:
+    for name in TABLES[EARLY:LATE]:
         loads[name].wait()
     row, lane = iotas()
     own = [(row // 2) == (lane // 64 + 2 * k2) for k2 in range(2)]
@@ -577,7 +588,7 @@
         source = got[0, u].reshape(16 * devices, 256)
         coeffs[u] = (fdot(tables["x_in"][...], source) * forward_scale).reshape(2, MX, 8, 256)
 
-        @pl.loop(0, 4)
+        @pl.loop(0, 4, unroll=PARTS)
         def _(part):
             half, local = part // 2, part % 2
             weight_copy(half, 2 * u + local).wait()
@@ -634,14 +645,15 @@
             lefts[index, k_half] = wide.T.astype(BF16)
 
     load_cot.wait()
-    ends[2][0]()
-    ends[3][0]()
-    to_lines(devices, got.at[1], tables["y_out"], tables["unorder"], blocks)
-
-    @pl.loop(0, lines // rows)
+    for name in TABLES[LATE:]:
+        loads[name].wait()
+    lines_of(1, ends[2:4])
+
+    @pl.loop(0, lines // rows, unroll=True)
     def _(block):
         line = pl.ds(pl.multiple_of(block * rows, rows), rows)
-        spectral[...] = fdot(blocks[block], tables["z_out"][...])
+        slot = block % 2
+        spectral[slot] = fdot(blocks[block], tables["z_out"][...])
 
         @pl.loop(0, groups, unroll=True)
         def _(group):
@@ -650,7 +662,7 @@
                 for i in range(8):
                     o = group * 8 + i
                     hidden = (
-                        spectral[here, i * 128 : (i + 1) * 128]
+                        spectral[slot, here, i * 128 : (i + 1) * 128]
                         + pointwise[
                             block,
                             pl.ds(pl.multiple_of(o * rows, rows), rows),
@@ -701,7 +713,7 @@
         modes[...] = fdot(tables["x_in"][...], source).reshape(2, MX, 8, 256)
         turned[...] = fdot(tables["x_turn"][...], source).reshape(2, MX, 8, 256)
 
-        @pl.loop(0, 4)
+        @pl.loop(0, 4, unroll=PARTS)
         def _(part):
             half, local = part // 2, part % 2
             span = pl.ds(pl.multiple_of(local * 128, 128), 128)
@@ -752,14 +764,13 @@
         weight_grad_block(
             weight_scale, lefts.at[index], pairs.at[index], weights.at[:, 2 * index : 2 * index + 2]
         )
-    ends[6][0]()
-    ends[7][0]()
-    to_lines(devices, got.at[3], tables["y_out"], tables["unorder"], blocks)
-
-    @pl.loop(0, lines // rows)
+    lines_of(3, ends[6:8])
+
+    @pl.loop(0, lines // rows, unroll=True)
     def _(block):
         line = pl.ds(pl.multiple_of(block * rows, rows), rows)
-        spectral[...] = fdot(blocks[block], tables["z_out"][...])
+        slot = block % 2
+        spectral[slot] = fdot(blocks[block], tables["z_out"][...])
 
         @pl.loop(0, groups, unroll=True)
         def _(group):
@@ -768,7 +779,7 @@
                 for i in range(8):
                     o = group * 8 + i
                     total = (
-                        spectral[here, i * 128 : (i + 1) * 128]
+                        spectral[slot, here, i * 128 : (i + 1) * 128]
                         + pointwise[
                             block,
                             pl.ds(pl.multiple_of(o * rows, rows), rows),
@@ -781,24 +792,32 @@
         end[1]()
 
 
-def to_lines(devices, back, y_out, unorder, blocks):
-    lines_u = [fdot(y_out[...], back[u].reshape(16 * devices, 256)).astype(BF16) for u in range(2)]
-    lines = lines_u[0].shape[0] // 8
+def to_lines(u, back, y_out, unorder, total):
+    values = fdot(y_out[...], back[u].reshape(-1, 256)).astype(BF16)
+    lines = values.shape[0] // 8
+    part = 0.0
+    for half in range(2):
+        rows = jnp.concatenate(
+            [values[(2 * i + half) * lines : (2 * i + half + 1) * lines] for i in range(4)], 0
+        )
+        first = (2 * half + u) * 256
+        part = part + fdot(rows, unorder[first : first + 256, :])
+    total[...] = part if u == 0 else total[...] + part
+
+
+def to_blocks(total, blocks):
+    size, wide = total.shape
+    lines, groups = size // 4, wide // 128
     for plane in range(2):
         for part in range(2):
-            pieces = []
-            for half in range(2):
-                first = ((plane * 2 + part) * 2 + half) * lines
-                pieces += [lines_u[u][first : first + lines] for u in range(2)]
-            rows = fdot(jnp.concatenate(pieces, 1), unorder[...]).astype(BF16)
-            groups = rows.shape[1] // 128
             for block in range(lines // 16):
+                first = (plane * 2 + part) * lines + block * 16
                 for group in range(groups):
                     blocks[
                         block,
                         (plane * groups + group) * 16 : (plane * groups + group + 1) * 16,
                         part * 128 : (part + 1) * 128,
-                    ] = rows[block * 16 : (block + 1) * 16, group * 128 : (group + 1) * 128]
+                    ] = total[first : first + 16, group * 128 : (group + 1) * 128].astype(BF16)
 
 
 def pair_tile(straight, other, low, direct):
@@ -903,7 +922,7 @@
             vmem(steps, channels * rows, planes * depth_len, dtype=F32),
             vmem(4 * lines, wide),
             vmem(steps, 2 * wide // 8, 256),
-            vmem(planes * channels * 2, 8 * depth_len, dtype=F32),
+            vmem(2, planes * channels * 2, 8 * depth_len, dtype=F32),
             vmem(steps, planes * channels * 2, 8 * depth_len),
             vmem(4, 2, devices, 16, 256),
             vmem(4, 2, devices, 16, 256),

time: 61.6 us -> 58.1 us (0.943)
  Pallas kernels: 60.7 us -> 57.1 us
    pallas_call x1, Pallas kernels: 53.5 us -> 49.9 us  [block_body(): pl.pallas_call(functools.partial(layer_kernel, devices, forward_scale, in...]
where the time goes in v4:
time: 58.1 us; the launch traced here: 57.9 us
  Pallas kernels  57.1 us (98%)
  between operations  0.8 us (1%)
    pallas_call x1, Pallas kernels, block_body(): pl.pallas_call(functools.partial(layer_kernel, devices, forward_scale, in...  49.9 us
    pallas_call x1, Pallas kernels, block_body(): pl.pallas_call(functools.partial(weight_grad_kernel, weight_scale), out_s...  7.2 us

profile of v4, /device:TPU:0, one launch (start us, length us, event | category | flops | bytes accessed | tf_op | source)
XLA Modules:
  0.0 57.9 jit_solution(13931748520689965616)
XLA Ops:
  0.6 49.9 %layer.1 = (bf16[64,2,64,128]{3,2,1,0:T(8,128)(2,1)S(1)}, bf16[64,2,64,128]{3,2,1,0:T(8,128)(2,1)S(1)}, bf16[2,16,32,64,128]{4,3,2,1,0:T(8,128)(2,1)S(1)}, bf16[...) custom-call(bf16[64,2,64,128]{3,2,1,0:T(8,128)(2,1)} %feat_hbm.1, bf16[64,2,64,128]{3,2,1,0:T(8,128)(2,1)} %cot_hbm.1, ...), custom_call_target="tpu_custom_call" | custom-call | tf_op jit(solution)/shard_map/layer/pallas_call | solution.py:906
  50.5 7.2 %weight_grad.1 = (bf16[64,2,64,128]{3,2,1,0:T(8,128)(2,1)}, bf16[64,2,64,128]{3,2,1,0:T(8,128)(2,1)}, bf16[2,16,32,64,128]{4,3,2,1,0:T(8,128)(2,1)}) custom-call(bf16[64,2,64,128]{3,2,1,0:T(8,128)(2,1)S(1)} %get-tuple-element.11.act_in, bf16[64,2,64,128]{3,2,1,0:T(8,128)(2,1)S(1)} %get-tuple-element.12.grad_in, ...), custom_call_target="tpu_custom_call" | custom-call | tf_op jit(solution)/shard_map/weight_grad/pallas_call | solution.py:944

commit v5 on v4

--- a/solution.py
+++ b/solution.py
@@ -364,32 +364,30 @@
 def swap_start(devices, sent, got, send_sem, recv_sem, stage):
     me, group = lax.axis_index("gx"), lax.axis_index("grp")
 
-    def copy(step):
-        target = lax.rem(me + step, devices)
+    def copy(source, landing, target):
         return pltpu.make_async_remote_copy(
-            src_ref=sent.at[target],
-            dst_ref=got.at[me],
-            send_sem=send_sem.at[stage, step],
-            recv_sem=recv_sem.at[stage, step],
+            src_ref=source,
+            dst_ref=landing,
+            send_sem=send_sem.at[stage],
+            recv_sem=recv_sem.at[stage],
             device_id=(group, target),
             device_id_type=MESH,
         )
 
-    @pl.loop(1, devices)
+    @pl.loop(1, devices, unroll=True)
     def _(step):
-        copy(step).start()
+        target = lax.rem(me + step, devices)
+        copy(sent.at[target], got.at[me], target).start()
 
     got[me] = sent[me]
+    others = pl.ds(0, devices - 1)
+    every = copy(sent.at[others], got.at[others], lax.rem(me + 1, devices))
 
     def finish():
-        @pl.loop(1, devices)
-        def _(step):
-            copy(step).wait_recv()
+        every.wait_recv()
 
     def drained():
-        @pl.loop(1, devices)
-        def _(step):
-            copy(step).wait_send()
+        every.wait_send()
 
     return finish, drained
 
@@ -933,8 +931,8 @@
             dma((4,)),
             dma((len(tables) + 1,)),
             dma((2, 4)),
-            dma((8, devices)),
-            dma((8, devices)),
+            dma((8,)),
+            dma((8,)),
         ],
         compiler_params=pltpu.CompilerParams(
             collective_id=0, has_side_effects=True, vmem_limit_bytes=40 * MB

time: 58.1 us -> 54.3 us (0.935)
  Pallas kernels: 57.1 us -> 53.2 us
    pallas_call x1, Pallas kernels: 49.9 us -> 46 us  [block_body(): pl.pallas_call(functools.partial(layer_kernel, devices, forward_scale, in...]
where the time goes in v5:
time: 54.3 us; the launch traced here: 54 us
  Pallas kernels  53.2 us (98%)
  between operations  0.8 us (1%)
    pallas_call x1, Pallas kernels, block_body(): pl.pallas_call(functools.partial(layer_kernel, devices, forward_scale, in...  46 us
    pallas_call x1, Pallas kernels, block_body(): pl.pallas_call(functools.partial(weight_grad_kernel, weight_scale), out_s...  7.2 us

profile of v5, /device:TPU:0, one launch (start us, length us, event | category | flops | bytes accessed | tf_op | source)
XLA Modules:
  0.0 54.0 jit_solution(18033257175115973067)
XLA Ops:
  0.6 46.0 %layer.1 = (bf16[64,2,64,128]{3,2,1,0:T(8,128)(2,1)S(1)}, bf16[64,2,64,128]{3,2,1,0:T(8,128)(2,1)S(1)}, bf16[2,16,32,64,128]{4,3,2,1,0:T(8,128)(2,1)S(1)}, bf16[...) custom-call(bf16[64,2,64,128]{3,2,1,0:T(8,128)(2,1)} %feat_hbm.1, bf16[64,2,64,128]{3,2,1,0:T(8,128)(2,1)} %cot_hbm.1, ...), custom_call_target="tpu_custom_call" | custom-call | tf_op jit(solution)/shard_map/layer/pallas_call | solution.py:904
  46.7 7.2 %weight_grad.1 = (bf16[64,2,64,128]{3,2,1,0:T(8,128)(2,1)}, bf16[64,2,64,128]{3,2,1,0:T(8,128)(2,1)}, bf16[2,16,32,64,128]{4,3,2,1,0:T(8,128)(2,1)}) custom-call(bf16[64,2,64,128]{3,2,1,0:T(8,128)(2,1)S(1)} %get-tuple-element.11.act_in, bf16[64,2,64,128]{3,2,1,0:T(8,128)(2,1)S(1)} %get-tuple-element.12.grad_in, ...), custom_call_target="tpu_custom_call" | custom-call | tf_op jit(solution)/shard_map/weight_grad/pallas_call | solution.py:942

commit v6 on v5

--- a/solution.py
+++ b/solution.py
@@ -349,7 +349,7 @@
     me, group = lax.axis_index("gx"), lax.axis_index("grp")
     barrier = pltpu.get_barrier_semaphore()
 
-    @pl.loop(1, devices)
+    @pl.loop(1, devices, unroll=True)
     def _(step):
         pl.semaphore_signal(
             barrier, inc=1, device_id=(group, lax.rem(me + step, devices)), device_id_type=MESH
@@ -463,7 +463,7 @@
 )
 EARLY = 3
 LATE = 5
-PARTS = 2
+PARTS = 4
 
 
 def layer_kernel(
@@ -482,7 +482,6 @@
     channels, planes, lines, depth_len = feat.shape
     groups = channels // 8
     rows = 16
-    arrived = greet(devices)
     pieces = feat_sem.shape[0]
     share = channels // pieces
 
@@ -500,6 +499,7 @@
         load_feat(piece).start()
     for name in TABLES[1:EARLY]:
         loads[name].start()
+    arrived = greet(devices)
     weight_copy = weight_copies(weights_hbm, weights, weight_sem)
     loads["z_in"].wait()
 

time: 54.3 us -> 53.8 us (level)
  no operation moved by 1% of the time
where the time goes in v6:
time: 53.8 us; the launch traced here: 53.5 us
  Pallas kernels  52.7 us (98%)
  between operations  0.8 us (1%)
    pallas_call x1, Pallas kernels, block_body(): pl.pallas_call(functools.partial(layer_kernel, devices, forward_scale, in...  45.5 us
    pallas_call x1, Pallas kernels, block_body(): pl.pallas_call(functools.partial(weight_grad_kernel, weight_scale), out_s...  7.2 us

profile of v6, /device:TPU:0, one launch (start us, length us, event | category | flops | bytes accessed | tf_op | source)
XLA Modules:
  0.0 53.5 jit_solution(33748581870891041)
XLA Ops:
  0.6 45.5 %layer.1 = (bf16[64,2,64,128]{3,2,1,0:T(8,128)(2,1)S(1)}, bf16[64,2,64,128]{3,2,1,0:T(8,128)(2,1)S(1)}, bf16[2,16,32,64,128]{4,3,2,1,0:T(8,128)(2,1)S(1)}, bf16[...) custom-call(bf16[64,2,64,128]{3,2,1,0:T(8,128)(2,1)} %feat_hbm.1, bf16[64,2,64,128]{3,2,1,0:T(8,128)(2,1)} %cot_hbm.1, ...), custom_call_target="tpu_custom_call" | custom-call | tf_op jit(solution)/shard_map/layer/pallas_call | solution.py:904
  46.1 7.2 %weight_grad.1 = (bf16[64,2,64,128]{3,2,1,0:T(8,128)(2,1)}, bf16[64,2,64,128]{3,2,1,0:T(8,128)(2,1)}, bf16[2,16,32,64,128]{4,3,2,1,0:T(8,128)(2,1)}) custom-call(bf16[64,2,64,128]{3,2,1,0:T(8,128)(2,1)S(1)} %get-tuple-element.11.act_in, bf16[64,2,64,128]{3,2,1,0:T(8,128)(2,1)S(1)} %get-tuple-element.12.grad_in, ...), custom_call_target="tpu_custom_call" | custom-call | tf_op jit(solution)/shard_map/weight_grad/pallas_call | solution.py:942
